TPU v7x, 32 devices: a whole 2x2x4 slice. The times are simulated.
32 devices in a mesh: grp: 2 (over y), ctx: 8 (over z, x), pair: 2 (over core).
Axes of the slice: x: 2, y: 2, z: 4, core: 2. Of those that a mesh axis runs over, the one named last changes fastest.
Arguments:
- normed_input: bfloat16 [4, 1024, 2688], P(('grp', 'pair'), 'ctx'), parts along dimension 0, may hold values from -6 to 6
- queries: bfloat16 [4, 1024, 2048], P(('grp', 'pair'), 'ctx'), parts along dimension 0, may hold values from -64 to 64
- keys: bfloat16 [4, 1024, 1024], P(('grp', 'pair'), 'ctx'), parts along dimension 0, may hold values from -64 to 64
- value_projection: bfloat16 [2688, 1024], P('ctx'), may hold values from -0.125 to 0.125
- adapter_down: bfloat16 [2688, 16], replicated, may hold values from -0.125 to 0.125
- adapter_up: bfloat16 [16, 1024], replicated, may hold values from -1.5 to 1.5
- output_gradient: bfloat16 [4, 1024, 2048], P(('grp', 'pair'), 'ctx'), parts along dimension 0, may hold values from -6 to 6
- policy_logprob: float32 [4, 1024], P(('grp', 'pair'), 'ctx'), parts along dimension 0, may hold values from -6 to 0
- reference_logprob: float32 [4, 1024], P(('grp', 'pair'), 'ctx'), parts along dimension 0, may hold values from -8 to 0
- token_pair_index: int32 [4, 1024], P(('grp', 'pair'), 'ctx'), parts along dimension 0, may hold values from 0 to 7, never falling along the last dimension, each value on 1 to 1017 neighbouring positions
Outputs:
- input_grad: bfloat16 [4, 1024, 2688], P(('grp', 'pair'), 'ctx'), parts along dimension 0
- query_grad: bfloat16 [4, 1024, 2048], P(('grp', 'pair'), 'ctx'), parts along dimension 0
- key_grad: bfloat16 [4, 1024, 1024], P(('grp', 'pair'), 'ctx'), parts along dimension 0
- down_gradient: float32 [5376, 16], P('grp'), parts along dimension 0
- up_gradient: float32 [32, 1024], P('grp'), parts along dimension 0
There are 2 independent parts, one for each index of `grp`. A program takes and returns all parts, laid end to end along the dimension named above; an argument that names none is the same for every part. Nothing has to cross between parts.
Inputs may be any that keep to these rules, and one draw needn't show every extreme that they name: `token_pair_index`: along each sequence the ids never fall; both sequences hold every id, each segment at most 1017 tokens and one exactly 1017.
All inputs are finite; a program needn't handle non-finite values.
Results may differ from a plain program's by a relative error of at most 0.03.
Values may be sent and summed in bfloat16 or wider, within the bound.
A program may use at most 128 MiB of HBM per device.

v0:
```python
import jax
import jax.numpy as jnp
from jax import lax
from jax.sharding import PartitionSpec as P

HEAD_SIZE = 128
WINDOW = 1024
SEGS = 8


DPO_BETA = 0.1
LOSS_SCALE = 256.0
ADAPTER_SCALE = 2.0
ATTN_SCALE = 168.0 ** (-0.5)
NEG_FILL = -1e30


def from_partner(shard, axis, stride):
    return lax.ppermute(shard, axis, [(i, i ^ 1 << stride) for i in range(lax.axis_size(axis))])


def shifted(block, axis, distance):
    devices = range(lax.axis_size(axis))
    route = [(i - distance, i) for i in devices if i - distance in devices]
    return lax.ppermute(block, axis, route)


def shards(
    normed_input,
    queries,
    keys,
    value_projection,
    adapter_down,
    adapter_up,
    output_gradient,
    policy_logprob,
    reference_logprob,
    token_pair_index,
):
    tok_rows = normed_input.shape[1]
    width_kv = keys.shape[2]
    kv_heads = width_kv // HEAD_SIZE
    group_size = queries.shape[2] // width_kv
    hidden_rows = normed_input[0]
    own_keys = keys[0]
    pair_index = lax.axis_index("pair")
    ctx_index = lax.axis_index("ctx")
    half_cols = width_kv // 2
    own_half = lax.dynamic_slice_in_dim(value_projection, pair_index * half_cols, half_cols, 1)
    rows_half = lax.all_gather(own_half, "ctx", axis=0, tiled=True)
    full_weight = lax.all_gather(rows_half, "pair", axis=1, tiled=True)
    rank_projection = jnp.dot(hidden_rows, adapter_down, preferred_element_type=jnp.float32).astype(
        jnp.bfloat16
    )
    values = (
        jnp.dot(hidden_rows, full_weight, preferred_element_type=jnp.float32)
        + ADAPTER_SCALE * jnp.dot(rank_projection, adapter_up, preferred_element_type=jnp.float32)
    ).astype(jnp.bfloat16)
    segment_labels = token_pair_index[0]
    seg_table = (segment_labels[:, None] == jnp.arange(SEGS, dtype=jnp.int32)[None, :]).astype(
        jnp.float32
    )
    log_gap = policy_logprob[0] - reference_logprob[0]
    part_diff = jnp.sum(seg_table * log_gap[:, None], 0)
    part_count = jnp.sum(seg_table, 0)
    own_diff, counts = lax.psum((part_diff, part_count), "ctx")
    other_diff = from_partner(own_diff, "pair", 0)
    direction = 1.0 - 2.0 * pair_index.astype(jnp.float32)
    margin = DPO_BETA * (direction * (own_diff - other_diff))
    coef = -direction * DPO_BETA * LOSS_SCALE * jax.nn.sigmoid(-margin)
    starts = jnp.cumsum(counts) - counts
    tok_start = jnp.sum(seg_table * starts[None, :], 1).astype(jnp.int32)
    token_coefficient = jnp.sum(seg_table * coef[None, :], 1)
    halo_blocks = WINDOW // tok_rows
    key_blocks = []
    value_blocks = []
    for distance in range(halo_blocks, 0, -1):
        got_keys, got_values = shifted((own_keys, values), "ctx", distance)
        key_blocks.append(got_keys)
        value_blocks.append(got_values)
    all_keys = jnp.concatenate(key_blocks + [own_keys], 0)
    all_values = jnp.concatenate(value_blocks + [values], 0)
    span = all_keys.shape[0]
    tpos = ctx_index * tok_rows + jnp.arange(tok_rows, dtype=jnp.int32)
    upos = ctx_index * tok_rows - WINDOW + jnp.arange(span, dtype=jnp.int32)
    allowed = (
        (upos[None, :] <= tpos[:, None])
        & (upos[None, :] > tpos[:, None] - WINDOW)
        & (upos[None, :] >= tok_start[:, None])
    )
    coef_rows = token_coefficient[None, :, None]
    query_heads = (
        queries[0].reshape(tok_rows, kv_heads, group_size, HEAD_SIZE).transpose(1, 0, 2, 3)
    )
    grad_heads = (
        output_gradient[0].reshape(tok_rows, kv_heads, group_size, HEAD_SIZE).transpose(1, 0, 2, 3)
    )
    key_heads = all_keys.reshape(span, kv_heads, HEAD_SIZE).transpose(1, 0, 2)
    value_heads = all_values.reshape(span, kv_heads, HEAD_SIZE).transpose(1, 0, 2)

    def per_head(operands):
        query_head, key_head, value_head, grad_head = operands
        scores = ATTN_SCALE * jnp.einsum(
            "tgd,ld->gtl", query_head, key_head, preferred_element_type=jnp.float32
        )
        masked = jnp.where(allowed[None], scores, NEG_FILL)
        row_max = jnp.max(masked, -1, keepdims=True)
        weights_exp = jnp.where(allowed[None], jnp.exp(masked - row_max), 0.0)
        attn_probs = weights_exp / jnp.sum(weights_exp, -1, keepdims=True)
        prob_grad = coef_rows * jnp.einsum(
            "tgd,ld->gtl", grad_head, value_head, preferred_element_type=jnp.float32
        )
        row_delta = jnp.sum(attn_probs * prob_grad, -1, keepdims=True)
        score_grad = (ATTN_SCALE * attn_probs * (prob_grad - row_delta)).astype(jnp.bfloat16)
        head_qgrad = jnp.einsum(
            "gtl,ld->tgd", score_grad, key_head, preferred_element_type=jnp.float32
        ).astype(jnp.bfloat16)
        head_kgrad = jnp.einsum(
            "gtl,tgd->ld", score_grad, query_head, preferred_element_type=jnp.float32
        )
        weighted = (attn_probs * coef_rows).astype(jnp.bfloat16)
        head_vgrad = jnp.einsum(
            "gtl,tgd->ld", weighted, grad_head, preferred_element_type=jnp.float32
        )
        return (head_qgrad, head_kgrad, head_vgrad)

    query_stack, key_stack, value_stack = lax.map(
        per_head, (query_heads, key_heads, value_heads, grad_heads)
    )
    query_grad = query_stack.transpose(1, 0, 2, 3).reshape(
        tok_rows, kv_heads * group_size * HEAD_SIZE
    )
    key_parts = key_stack.transpose(1, 0, 2).reshape(span, width_kv)
    value_parts = value_stack.transpose(1, 0, 2).reshape(span, width_kv)
    key_total = key_parts[WINDOW:]
    value_total = value_parts[WINDOW:]
    for distance in range(1, halo_blocks + 1):
        block_start = (halo_blocks - distance) * tok_rows
        send_keys = key_parts[block_start : block_start + tok_rows].astype(jnp.bfloat16)
        send_values = value_parts[block_start : block_start + tok_rows].astype(jnp.bfloat16)
        back_keys, back_values = shifted((send_keys, send_values), "ctx", -distance)
        key_total = key_total + back_keys.astype(jnp.float32)
        value_total = value_total + back_values.astype(jnp.float32)
    key_grad = key_total.astype(jnp.bfloat16)
    value_gradient = value_total.astype(jnp.bfloat16)
    rank_middle = jnp.einsum(
        "sj,zj->sz", value_gradient, adapter_up, preferred_element_type=jnp.float32
    ).astype(jnp.bfloat16)
    input_grad = (
        jnp.einsum("tk,dk->td", value_gradient, full_weight, preferred_element_type=jnp.float32)
        + ADAPTER_SCALE
        * jnp.einsum("pb,wb->pw", rank_middle, adapter_down, preferred_element_type=jnp.float32)
    ).astype(jnp.bfloat16)
    up_factor = ADAPTER_SCALE * jnp.einsum(
        "tr,tk->rk", rank_projection, value_gradient, preferred_element_type=jnp.float32
    )
    down_factor = ADAPTER_SCALE * jnp.einsum(
        "td,tr->dr", hidden_rows, rank_middle, preferred_element_type=jnp.float32
    )
    down_gradient, up_gradient = lax.psum((down_factor, up_factor), ("ctx", "pair"))
    return (input_grad[None], query_grad[None], key_grad[None], down_gradient, up_gradient)


def solution(mesh):
    return jax.shard_map(
        shards,
        mesh=mesh,
        in_specs=(
            P(("grp", "pair"), "ctx", None),
            P(("grp", "pair"), "ctx", None),
            P(("grp", "pair"), "ctx", None),
            P("ctx", None),
            P(),
            P(),
            P(("grp", "pair"), "ctx", None),
            P(("grp", "pair"), "ctx"),
            P(("grp", "pair"), "ctx"),
            P(("grp", "pair"), "ctx"),
        ),
        out_specs=(
            P(("grp", "pair"), "ctx", None),
            P(("grp", "pair"), "ctx", None),
            P(("grp", "pair"), "ctx", None),
            P("grp", None),
            P("grp", None),
        ),
        check_vma=False,
    )
```

profile of v0, /device:TPU:27, one launch (start us, length us, event | category | flops | bytes accessed | tf_op | source)
XLA Modules:
  0.0 452.3 jit_solution(16031757888208835869)
XLA Ops:
  7.3 1.8 constant_dynamic-slice_fusion
  9.2 56.3 %all-gather.3.cloned.1.call-done = bf16[2688,512]{1,0:T(8,128)(2,1)} async-done(((bf16[336,512]{1,0:T(8,128)(2,1)}), bf16[2688,512]{1,0:T(8,128)(2,1)}) %all-gather.3.cloned.1.call-update) | async-done | bytes 2752528 | tf_op jit(solution)/shard_map/all_gather | solution.py:50
  71.2 23.9 %all-reduce.1 = (f32[8]{0:T(128)S(1)}, f32[8]{0:T(128)S(1)}) all-reduce(f32[8]{0:T(128)S(1)} %get-tuple-element.122, f32[8]{0:T(128)S(1)} %get-tuple-element.123), channel_id=1, replica_groups=mesh['grp'=2,'ctx'=8,'pair'=2] {'ctx'}, use_global_device_ids=true, to_apply=%region_1.0 | all-reduce | flops 16 | bytes 128 | tf_op jit(solution)/shard_map/psum | solution.py:66
  95.1 5.4 %collective-permute-start.8 = (f32[8]{0:T(128)S(1)}, f32[8]{0:T(128)S(1)}, u32[]{:S(2)}, u32[]{:S(2)}) collective-permute-start(f32[8]{0:T(128)S(1)} %get-tuple-element.153), channel_id=1, source_target_pairs={{0,1},{1,0},{2,3},{3,2},{4,5},{5,4},{6,7},{7,6},{8,9},{9,8},{10,11... | collective-permute-start | bytes 104 | tf_op jit(solution)/shard_map/ppermute | solution.py:19
  109.5 15.7 %collective-permute-done.3 = bf16[128,1024]{0,1:T(8,128)(2,1)S(1)} collective-permute-done((bf16[128,1024]{0,1:T(8,128)(2,1)S(1)}, bf16[128,1024]{0,1:T(8,128)(2,1)S(1)}, u32[]{:S(2)}, u32[]{:S(2)}) %collective-permute-start.3) | collective-permute-done | bytes 262176 | tf_op jit(solution)/shard_map/ppermute | solution.py:25
  125.9 5.2 %collective-permute-done.4 = bf16[128,1024]{0,1:T(8,128)(2,1)S(1)} collective-permute-done((bf16[128,1024]{0,1:T(8,128)(2,1)S(1)}, bf16[128,1024]{0,1:T(8,128)(2,1)S(1)}, u32[]{:S(2)}, u32[]{:S(2)}) %collective-permute-start.4) | collective-permute-done | bytes 262176 | tf_op jit(solution)/shard_map/ppermute | solution.py:25
  132.7 3.5 convolution_bitcast_fusion.2
  145.9 3.9 collective-permute-done.10
  152.5 27.0 %collective-permute-done.12 = bf16[128,1024]{1,0:T(8,128)(2,1)S(1)} collective-permute-done((bf16[128,1024]{1,0:T(8,128)(2,1)S(1)}, bf16[128,1024]{1,0:T(8,128)(2,1)S(1)}, u32[]{:S(2)}, u32[]{:S(2)}) %collective-permute-start.12) | collective-permute-done | bytes 262176 | tf_op jit(solution)/shard_map/ppermute | solution.py:25
  179.5 6.1 %collective-permute-done.13 = bf16[128,1024]{1,0:T(8,128)(2,1)S(1)} collective-permute-done((bf16[128,1024]{1,0:T(8,128)(2,1)S(1)}, bf16[128,1024]{1,0:T(8,128)(2,1)S(1)}, u32[]{:S(2)}, u32[]{:S(2)}) %collective-permute-start.13) | collective-permute-done | bytes 262176 | tf_op jit(solution)/shard_map/ppermute | solution.py:25
  185.8 1.8 bitcast_bitcast_fusion
  187.6 75.4 %while.15 = (s32[]{:T(128)}, bf16[8,128,2,128]{1,3,2,0:T(8,128)(2,1)}, f32[8,1152,128]{2,1,0:T(8,128)}, f32[8,1152,128]{1,2,0:T(8,128)}, bf16[8,1152,128]{1,2,0:...) while((s32[]{:T(128)}, ...), condition=%wide.region_11.12_spmd.clone, body=%wide.region_7.11_spmd.clone.sunk | while | flops 459950336 | bytes 11177101 | solution.py:127
  191.1 1.9 fusion.126
  194.1 2.9 fusion.128
  197.2 1.7 fusion.125
  200.6 1.9 fusion.126
  203.5 2.8 fusion.128
  209.9 1.9 fusion.126
  212.9 2.9 fusion.128
  219.3 1.9 fusion.126
  222.4 2.9 fusion.128
  225.5 1.7 fusion.125
  228.8 1.9 fusion.126
  231.8 2.9 fusion.128
  238.3 1.9 fusion.126
  241.3 2.8 fusion.128
  244.4 1.7 fusion.125
  247.7 1.9 fusion.126
  250.7 2.8 fusion.128
  253.8 1.7 fusion.125
  257.1 1.9 fusion.126
  260.1 2.8 fusion.128
  263.0 2.7 bitcast_convert_fusion.1
  268.5 9.4 %collective-permute-start.17 = (bf16[128,1024]{0,1:T(8,128)(2,1)}, bf16[128,1024]{0,1:T(8,128)(2,1)}, u32[]{:S(2)}, u32[]{:S(2)}) collective-permute-start(bf16[128,1024]{0,1:T(8,128)(2,1)} %bitcast.25), channel_id=1, source_target_pairs={{2,0},{4,2},{6,4},{8,6},{10,8},{12,10},{14,12},{3,1},{5,3},{7,5},{... | collective-permute-start | bytes 786440 | tf_op jit(solution)/shard_map/ppermute | solution.py:25
  277.8 2.0 collective-permute-start.23
  279.8 2.7 bitcast_convert_fusion
  282.5 2.0 copy.72
  294.4 3.8 collective-permute-done.21
  298.2 2.0 collective-permute-start.27
  300.2 3.6 collective-permute-done.20
  303.8 13.9 %collective-permute-start.28 = (bf16[128,1024]{1,0:T(8,128)(2,1)S(1)}, bf16[128,1024]{1,0:T(8,128)(2,1)}, u32[]{:S(2)}, u32[]{:S(2)}) collective-permute-start(bf16[128,1024]{1,0:T(8,128)(2,1)S(1)} %bitcast.303), channel_id=1, source_target_pairs={{8,0},{10,2},{12,4},{14,6},{9,1},{11,3},{13,5},{15,7},{24,16},{26,... | collective-permute-start | bytes 786440 | tf_op jit(solution)/shard_map/ppermute | solution.py:25
  317.7 8.1 %collective-permute-start.29 = (bf16[128,1024]{1,0:T(8,128)(2,1)S(1)}, bf16[128,1024]{1,0:T(8,128)(2,1)}, u32[]{:S(2)}, u32[]{:S(2)}) collective-permute-start(bf16[128,1024]{1,0:T(8,128)(2,1)S(1)} %bitcast.302), channel_id=1, source_target_pairs={{10,0},{12,2},{14,4},{11,1},{13,3},{15,5},{26,16},{28,18},{30,20},... | collective-permute-start | bytes 786440 | tf_op jit(solution)/shard_map/ppermute | solution.py:25
  325.8 2.0 collective-permute-start.30
  333.5 2.5 collective-permute-start.25
  336.0 5.4 %fusion.57 = bf16[1,128,2688]{2,1,0:T(8,128)(2,1)} fusion(f32[128,2688]{1,0:T(8,128)S(1)} %convolution_multiply_fusion.2, bf16[128,1024]{0,1:T(8,128)(2,1)S(1)} %fusion.79, bf16[2688,1024]{1,0:T(8,128)(2,1)} %all-gather.5.cloned.1.call-done), kind=kOutput, calls=%fused_computation.51 | convolution fusion | flops 705331200 | bytes 7831552 | tf_op jit(solution)/shard_map/tk,dk->td/dot_general | solution.py:150
  343.0 5.6 %collective-permute-done.31 = bf16[128,1024]{1,0:T(8,128)(2,1)S(1)} collective-permute-done((bf16[128,1024]{1,0:T(8,128)(2,1)S(1)}, bf16[128,1024]{1,0:T(8,128)(2,1)S(1)}, u32[]{:S(2)}, u32[]{:S(2)}) %collective-permute-start.31) | collective-permute-done | bytes 262176 | tf_op jit(solution)/shard_map/ppermute | solution.py:25
  348.7 2.5 fusion.80
  351.1 91.6 %all-reduce.4.cloned.1.call-done = (f32[2688,16]{0,1:T(8,128)}, f32[16,1024]{1,0:T(8,128)}) async-done(((f32[2688,16]{0,1:T(8,128)}, f32[16,1024]{1,0:T(8,128)}), (f32[2688,16]{0,1:T(8,128)}, f32[16,1024]{1,0:T(8,128)})) %all-reduce.4.cloned.1.call-update) | async-done | bytes 237584 | tf_op jit(solution)/shard_map/psum | solution.py:160
  (164 shorter events, 82.7 us)
Async XLA Ops:
  7.2 94.1 %copy-start = (bf16[1,128,2688]{2,1,0:T(8,128)(2,1)S(1)}, bf16[1,128,2688]{2,1,0:T(8,128)(2,1)}, u32[]{:S(2)}) copy-start(bf16[1,128,2688]{2,1,0:T(8,128)(2,1)} %param.12) | copy-start | bytes 2064388
  7.2 58.4 %copy-start.4 = (bf16[1,128,1024]{2,1,0:T(8,128)(2,1)S(1)}, bf16[1,128,1024]{2,1,0:T(8,128)(2,1)}, u32[]{:S(2)}) copy-start(bf16[1,128,1024]{2,1,0:T(8,128)(2,1)} %param.14) | copy-start | bytes 786436
  7.2 63.8 %copy-start.8 = (f32[1,128]{1,0:T(1,128)S(1)}, f32[1,128]{1,0:T(1,128)}, u32[]{:S(2)}) copy-start(f32[1,128]{1,0:T(1,128)} %param.20) | copy-start | bytes 1540
  7.2 63.8 %copy-start.7 = (f32[1,128]{1,0:T(1,128)S(1)}, f32[1,128]{1,0:T(1,128)}, u32[]{:S(2)}) copy-start(f32[1,128]{1,0:T(1,128)} %param.19) | copy-start | bytes 1540
  7.2 63.8 %copy-start.6 = (s32[1,128]{1,0:T(1,128)S(1)}, s32[1,128]{1,0:T(1,128)}, u32[]{:S(2)}) copy-start(s32[1,128]{1,0:T(1,128)} %param.21) | copy-start | bytes 1540
  7.2 93.3 %copy-start.1 = (bf16[1,128,2048]{2,1,0:T(8,128)(2,1)S(1)}, bf16[1,128,2048]{2,1,0:T(8,128)(2,1)}, u32[]{:S(2)}) copy-start(bf16[1,128,2048]{2,1,0:T(8,128)(2,1)} %param.13) | copy-start | bytes 1572868
  7.2 58.3 %all-gather.3.cloned.1.call-start = ((), (), s32[]{:S(2)}) async-start(), calls=%async_computation | async-start | bytes 3096576 | tf_op jit(solution)/shard_map/all_gather | solution.py:50
  9.1 91.7 %copy-start.2 = (bf16[1,128,2048]{2,1,0:T(8,128)(2,1)S(1)}, bf16[1,128,2048]{2,1,0:T(8,128)(2,1)}, u32[]{:S(2)}) copy-start(bf16[1,128,2048]{2,1,0:T(8,128)(2,1)} %param.18) | copy-start | bytes 1572868
  9.2 123.5 %all-gather.5.cloned.1.call-start = ((), (), s32[]{:S(2)}) async-start(), calls=%async_computation.1 | async-start | bytes 8257536 | tf_op jit(solution)/shard_map/all_gather | solution.py:51
  65.5 35.7 %copy-start.3 = (bf16[2688,16]{0,1:T(8,128)(2,1)S(1)}, bf16[2688,16]{0,1:T(8,128)(2,1)}, u32[]{:S(2)}) copy-start(bf16[2688,16]{0,1:T(8,128)(2,1)} %param.16) | copy-start | bytes 258052
  65.6 377.2 %all-reduce.4.cloned.1.call-start = ((), (), s32[]{:S(2)}) async-start(), calls=%async_computation.2 | async-start | bytes 475136 | tf_op jit(solution)/shard_map/psum | solution.py:160
  65.8 73.4 %collective-permute-start.7 = (bf16[128,1024]{0,1:T(8,128)(2,1)S(1)}, bf16[128,1024]{0,1:T(8,128)(2,1)S(1)}, u32[]{:S(2)}, u32[]{:S(2)}) collective-permute-start(bf16[128,1024]{0,1:T(8,128)(2,1)S(1)} %bitcast.280), channel_id=1, source_target_pairs={{0,2},{2,4},{4,6},{6,8},{8,10},{10,12},{12,14},{1,3},{3,5},{5,7},{... | collective-permute-start | bytes 786440 | tf_op jit(solution)/shard_map/ppermute | solution.py:25
  67.1 70.0 %collective-permute-start.6 = (bf16[128,1024]{0,1:T(8,128)(2,1)S(1)}, bf16[128,1024]{0,1:T(8,128)(2,1)S(1)}, u32[]{:S(2)}, u32[]{:S(2)}) collective-permute-start(bf16[128,1024]{0,1:T(8,128)(2,1)S(1)} %bitcast.281), channel_id=1, source_target_pairs={{0,4},{2,6},{4,8},{6,10},{8,12},{10,14},{1,5},{3,7},{5,9},{7,11},{... | collective-permute-start | bytes 786440 | tf_op jit(solution)/shard_map/ppermute | solution.py:25
  68.4 39.1 %collective-permute-start.2 = (bf16[128,1024]{0,1:T(8,128)(2,1)S(1)}, bf16[128,1024]{0,1:T(8,128)(2,1)S(1)}, u32[]{:S(2)}, u32[]{:S(2)}) collective-permute-start(bf16[128,1024]{0,1:T(8,128)(2,1)S(1)} %bitcast.282), channel_id=1, source_target_pairs={{0,12},{2,14},{1,13},{3,15},{16,28},{18,30},{17,29},{19,31}} | collective-permute-start | bytes 786440 | tf_op jit(solution)/shard_map/ppermute | solution.py:25
  69.7 34.8 %collective-permute-start.1 = (bf16[128,1024]{0,1:T(8,128)(2,1)S(1)}, bf16[128,1024]{0,1:T(8,128)(2,1)}, u32[]{:S(2)}, u32[]{:S(2)}) collective-permute-start(bf16[128,1024]{0,1:T(8,128)(2,1)S(1)} %bitcast.283), channel_id=1, source_target_pairs={{0,14},{1,15},{16,30},{17,31}} | collective-permute-start | bytes 786440 | tf_op jit(solution)/shard_map/ppermute | solution.py:25
  95.1 6.5 %collective-permute-start.8 = (f32[8]{0:T(128)S(1)}, f32[8]{0:T(128)S(1)}, u32[]{:S(2)}, u32[]{:S(2)}) collective-permute-start(f32[8]{0:T(128)S(1)} %get-tuple-element.153), channel_id=1, source_target_pairs={{0,1},{1,0},{2,3},{3,2},{4,5},{5,4},{6,7},{7,6},{8,9},{9,8},{10,11... | collective-permute-start | bytes 104 | tf_op jit(solution)/shard_map/ppermute | solution.py:19
  101.6 0.8 collective-permute-start
  102.4 22.8 %collective-permute-start.3 = (bf16[128,1024]{0,1:T(8,128)(2,1)S(1)}, bf16[128,1024]{0,1:T(8,128)(2,1)S(1)}, u32[]{:S(2)}, u32[]{:S(2)}) collective-permute-start(bf16[128,1024]{0,1:T(8,128)(2,1)S(1)} %bitcast.285), channel_id=1, source_target_pairs={{0,10},{2,12},{4,14},{1,11},{3,13},{5,15},{16,26},{18,28},{20,30},... | collective-permute-start | bytes 786440 | tf_op jit(solution)/shard_map/ppermute | solution.py:25
  104.5 26.7 %collective-permute-start.4 = (bf16[128,1024]{0,1:T(8,128)(2,1)S(1)}, bf16[128,1024]{0,1:T(8,128)(2,1)S(1)}, u32[]{:S(2)}, u32[]{:S(2)}) collective-permute-start(bf16[128,1024]{0,1:T(8,128)(2,1)S(1)} %bitcast.286), channel_id=1, source_target_pairs={{0,8},{2,10},{4,12},{6,14},{1,9},{3,11},{5,13},{7,15},{16,24},{18,... | collective-permute-start | bytes 786440 | tf_op jit(solution)/shard_map/ppermute | solution.py:25
  107.5 24.4 %collective-permute-start.5 = (bf16[128,1024]{0,1:T(8,128)(2,1)S(1)}, bf16[128,1024]{0,1:T(8,128)(2,1)S(1)}, u32[]{:S(2)}, u32[]{:S(2)}) collective-permute-start(bf16[128,1024]{0,1:T(8,128)(2,1)S(1)} %bitcast.287), channel_id=1, source_target_pairs={{0,6},{2,8},{4,10},{6,12},{8,14},{1,7},{3,9},{5,11},{7,13},{9,15},... | collective-permute-start | bytes 786440 | tf_op jit(solution)/shard_map/ppermute | solution.py:25
  132.7 3.5 copy-start.5
  136.4 8.2 %collective-permute-start.9 = (bf16[128,1024]{1,0:T(8,128)(2,1)S(1)}, bf16[128,1024]{1,0:T(8,128)(2,1)S(1)}, u32[]{:S(2)}, u32[]{:S(2)}) collective-permute-start(bf16[128,1024]{1,0:T(8,128)(2,1)S(1)} %fusion.60), channel_id=1, source_target_pairs={} | collective-permute-start | bytes 786440 | tf_op jit(solution)/shard_map/ppermute | solution.py:25
  137.9 12.0 %collective-permute-start.10 = (bf16[128,1024]{1,0:T(8,128)(2,1)S(1)}, bf16[128,1024]{1,0:T(8,128)(2,1)S(1)}, u32[]{:S(2)}, u32[]{:S(2)}) collective-permute-start(bf16[128,1024]{1,0:T(8,128)(2,1)S(1)} %fusion.60), channel_id=1, source_target_pairs={{0,14},{1,15},{16,30},{17,31}} | collective-permute-start | bytes 786440 | tf_op jit(solution)/shard_map/ppermute | solution.py:25
  139.9 11.2 %collective-permute-start.11 = (bf16[128,1024]{1,0:T(8,128)(2,1)S(1)}, bf16[128,1024]{1,0:T(8,128)(2,1)S(1)}, u32[]{:S(2)}, u32[]{:S(2)}) collective-permute-start(bf16[128,1024]{1,0:T(8,128)(2,1)S(1)} %fusion.60), channel_id=1, source_target_pairs={{0,12},{2,14},{1,13},{3,15},{16,28},{18,30},{17,29},{19,31}} | collective-permute-start | bytes 786440 | tf_op jit(solution)/shard_map/ppermute | solution.py:25
  142.0 43.7 %collective-permute-start.16 = (bf16[128,1024]{1,0:T(8,128)(2,1)S(1)}, bf16[128,1024]{1,0:T(8,128)(2,1)S(1)}, u32[]{:S(2)}, u32[]{:S(2)}) collective-permute-start(bf16[128,1024]{1,0:T(8,128)(2,1)S(1)} %fusion.60), channel_id=1, source_target_pairs={{0,2},{2,4},{4,6},{6,8},{8,10},{10,12},{12,14},{1,3},{3,5},{5,7},{... | collective-permute-start | bytes 786440 | tf_op jit(solution)/shard_map/ppermute | solution.py:25
  143.3 42.4 %collective-permute-start.15 = (bf16[128,1024]{1,0:T(8,128)(2,1)S(1)}, bf16[128,1024]{1,0:T(8,128)(2,1)S(1)}, u32[]{:S(2)}, u32[]{:S(2)}) collective-permute-start(bf16[128,1024]{1,0:T(8,128)(2,1)S(1)} %fusion.60), channel_id=1, source_target_pairs={{0,4},{2,6},{4,8},{6,10},{8,12},{10,14},{1,5},{3,7},{5,9},{7,11},{... | collective-permute-start | bytes 786440 | tf_op jit(solution)/shard_map/ppermute | solution.py:25
  144.6 34.9 %collective-permute-start.12 = (bf16[128,1024]{1,0:T(8,128)(2,1)S(1)}, bf16[128,1024]{1,0:T(8,128)(2,1)S(1)}, u32[]{:S(2)}, u32[]{:S(2)}) collective-permute-start(bf16[128,1024]{1,0:T(8,128)(2,1)S(1)} %fusion.60), channel_id=1, source_target_pairs={{0,10},{2,12},{4,14},{1,11},{3,13},{5,15},{16,26},{18,28},{20,30},... | collective-permute-start | bytes 786440 | tf_op jit(solution)/shard_map/ppermute | solution.py:25
  149.8 35.7 %collective-permute-start.13 = (bf16[128,1024]{1,0:T(8,128)(2,1)S(1)}, bf16[128,1024]{1,0:T(8,128)(2,1)S(1)}, u32[]{:S(2)}, u32[]{:S(2)}) collective-permute-start(bf16[128,1024]{1,0:T(8,128)(2,1)S(1)} %fusion.60), channel_id=1, source_target_pairs={{0,8},{2,10},{4,12},{6,14},{1,9},{3,11},{5,13},{7,15},{16,24},{18,... | collective-permute-start | bytes 786440 | tf_op jit(solution)/shard_map/ppermute | solution.py:25
  151.2 34.4 %collective-permute-start.14 = (bf16[128,1024]{1,0:T(8,128)(2,1)S(1)}, bf16[128,1024]{1,0:T(8,128)(2,1)S(1)}, u32[]{:S(2)}, u32[]{:S(2)}) collective-permute-start(bf16[128,1024]{1,0:T(8,128)(2,1)S(1)} %fusion.60), channel_id=1, source_target_pairs={{0,6},{2,8},{4,10},{6,12},{8,14},{1,7},{3,9},{5,11},{7,13},{9,15},... | collective-permute-start | bytes 786440 | tf_op jit(solution)/shard_map/ppermute | solution.py:25
  267.1 21.2 %collective-permute-start.24 = (bf16[128,1024]{0,1:T(8,128)(2,1)}, bf16[128,1024]{0,1:T(8,128)(2,1)}, u32[]{:S(2)}, u32[]{:S(2)}) collective-permute-start(bf16[128,1024]{0,1:T(8,128)(2,1)} %bitcast.32), channel_id=1, source_target_pairs={} | collective-permute-start | bytes 786440 | tf_op jit(solution)/shard_map/ppermute | solution.py:25
  268.5 21.2 %collective-permute-start.17 = (bf16[128,1024]{0,1:T(8,128)(2,1)}, bf16[128,1024]{0,1:T(8,128)(2,1)}, u32[]{:S(2)}, u32[]{:S(2)}) collective-permute-start(bf16[128,1024]{0,1:T(8,128)(2,1)} %bitcast.25), channel_id=1, source_target_pairs={{2,0},{4,2},{6,4},{8,6},{10,8},{12,10},{14,12},{3,1},{5,3},{7,5},{... | collective-permute-start | bytes 786440 | tf_op jit(solution)/shard_map/ppermute | solution.py:25
  277.8 13.1 %collective-permute-start.23 = (bf16[128,1024]{0,1:T(8,128)(2,1)}, bf16[128,1024]{0,1:T(8,128)(2,1)}, u32[]{:S(2)}, u32[]{:S(2)}) collective-permute-start(bf16[128,1024]{0,1:T(8,128)(2,1)} %bitcast.31), channel_id=1, source_target_pairs={{14,0},{15,1},{30,16},{31,17}} | collective-permute-start | bytes 786440 | tf_op jit(solution)/shard_map/ppermute | solution.py:25
  285.7 7.4 %collective-permute-start.22 = (bf16[128,1024]{0,1:T(8,128)(2,1)}, bf16[128,1024]{0,1:T(8,128)(2,1)S(1)}, u32[]{:S(2)}, u32[]{:S(2)}) collective-permute-start(bf16[128,1024]{0,1:T(8,128)(2,1)} %bitcast.294), channel_id=1, source_target_pairs={{12,0},{14,2},{13,1},{15,3},{28,16},{30,18},{29,17},{31,19}} | collective-permute-start | bytes 786440 | tf_op jit(solution)/shard_map/ppermute | solution.py:25
  287.0 11.2 %collective-permute-start.21 = (bf16[128,1024]{0,1:T(8,128)(2,1)}, bf16[128,1024]{0,1:T(8,128)(2,1)S(1)}, u32[]{:S(2)}, u32[]{:S(2)}) collective-permute-start(bf16[128,1024]{0,1:T(8,128)(2,1)} %bitcast.293), channel_id=1, source_target_pairs={{10,0},{12,2},{14,4},{11,1},{13,3},{15,5},{26,16},{28,18},{30,20},... | collective-permute-start | bytes 786440 | tf_op jit(solution)/shard_map/ppermute | solution.py:25
  288.3 15.5 %collective-permute-start.20 = (bf16[128,1024]{0,1:T(8,128)(2,1)}, bf16[128,1024]{0,1:T(8,128)(2,1)S(1)}, u32[]{:S(2)}, u32[]{:S(2)}) collective-permute-start(bf16[128,1024]{0,1:T(8,128)(2,1)} %bitcast.292), channel_id=1, source_target_pairs={{8,0},{10,2},{12,4},{14,6},{9,1},{11,3},{13,5},{15,7},{24,16},{26,... | collective-permute-start | bytes 786440 | tf_op jit(solution)/shard_map/ppermute | solution.py:25
  289.6 28.0 %collective-permute-start.19 = (bf16[128,1024]{0,1:T(8,128)(2,1)}, bf16[128,1024]{0,1:T(8,128)(2,1)S(1)}, u32[]{:S(2)}, u32[]{:S(2)}) collective-permute-start(bf16[128,1024]{0,1:T(8,128)(2,1)} %bitcast.291), channel_id=1, source_target_pairs={{6,0},{8,2},{10,4},{12,6},{14,8},{7,1},{9,3},{11,5},{13,7},{15,9},... | collective-permute-start | bytes 786440 | tf_op jit(solution)/shard_map/ppermute | solution.py:25
  291.0 34.8 %collective-permute-start.18 = (bf16[128,1024]{0,1:T(8,128)(2,1)S(1)}, bf16[128,1024]{0,1:T(8,128)(2,1)S(1)}, u32[]{:S(2)}, u32[]{:S(2)}) collective-permute-start(bf16[128,1024]{0,1:T(8,128)(2,1)S(1)} %bitcast.290), channel_id=1, source_target_pairs={{4,0},{6,2},{8,4},{10,6},{12,8},{14,10},{5,1},{7,3},{9,5},{11,7},{... | collective-permute-start | bytes 786440 | tf_op jit(solution)/shard_map/ppermute | solution.py:25
  293.1 38.3 %collective-permute-start.26 = (bf16[128,1024]{1,0:T(8,128)(2,1)S(1)}, bf16[128,1024]{1,0:T(8,128)(2,1)S(1)}, u32[]{:S(2)}, u32[]{:S(2)}) collective-permute-start(bf16[128,1024]{1,0:T(8,128)(2,1)S(1)} %bitcast.305), channel_id=1, source_target_pairs={{4,0},{6,2},{8,4},{10,6},{12,8},{14,10},{5,1},{7,3},{9,5},{11,7},{... | collective-permute-start | bytes 786440 | tf_op jit(solution)/shard_map/ppermute | solution.py:25
  298.2 34.6 %collective-permute-start.27 = (bf16[128,1024]{1,0:T(8,128)(2,1)S(1)}, bf16[128,1024]{1,0:T(8,128)(2,1)}, u32[]{:S(2)}, u32[]{:S(2)}) collective-permute-start(bf16[128,1024]{1,0:T(8,128)(2,1)S(1)} %bitcast.304), channel_id=1, source_target_pairs={{6,0},{8,2},{10,4},{12,6},{14,8},{7,1},{9,3},{11,5},{13,7},{15,9},... | collective-permute-start | bytes 786440 | tf_op jit(solution)/shard_map/ppermute | solution.py:25
  303.8 29.7 %collective-permute-start.28 = (bf16[128,1024]{1,0:T(8,128)(2,1)S(1)}, bf16[128,1024]{1,0:T(8,128)(2,1)}, u32[]{:S(2)}, u32[]{:S(2)}) collective-permute-start(bf16[128,1024]{1,0:T(8,128)(2,1)S(1)} %bitcast.303), channel_id=1, source_target_pairs={{8,0},{10,2},{12,4},{14,6},{9,1},{11,3},{13,5},{15,7},{24,16},{26,... | collective-permute-start | bytes 786440 | tf_op jit(solution)/shard_map/ppermute | solution.py:25
  317.7 23.7 %collective-permute-start.29 = (bf16[128,1024]{1,0:T(8,128)(2,1)S(1)}, bf16[128,1024]{1,0:T(8,128)(2,1)}, u32[]{:S(2)}, u32[]{:S(2)}) collective-permute-start(bf16[128,1024]{1,0:T(8,128)(2,1)S(1)} %bitcast.302), channel_id=1, source_target_pairs={{10,0},{12,2},{14,4},{11,1},{13,3},{15,5},{26,16},{28,18},{30,20},... | collective-permute-start | bytes 786440 | tf_op jit(solution)/shard_map/ppermute | solution.py:25
  325.8 17.3 %collective-permute-start.30 = (bf16[128,1024]{1,0:T(8,128)(2,1)S(1)}, bf16[128,1024]{1,0:T(8,128)(2,1)}, u32[]{:S(2)}, u32[]{:S(2)}) collective-permute-start(bf16[128,1024]{1,0:T(8,128)(2,1)S(1)} %bitcast.300), channel_id=1, source_target_pairs={{12,0},{14,2},{13,1},{15,3},{28,16},{30,18},{29,17},{31,19}} | collective-permute-start | bytes 786440 | tf_op jit(solution)/shard_map/ppermute | solution.py:25
  331.4 17.2 %collective-permute-start.31 = (bf16[128,1024]{1,0:T(8,128)(2,1)S(1)}, bf16[128,1024]{1,0:T(8,128)(2,1)S(1)}, u32[]{:S(2)}, u32[]{:S(2)}) collective-permute-start(bf16[128,1024]{1,0:T(8,128)(2,1)S(1)} %bitcast.299), channel_id=1, source_target_pairs={{14,0},{15,1},{30,16},{31,17}} | collective-permute-start | bytes 786440 | tf_op jit(solution)/shard_map/ppermute | solution.py:25
  332.8 15.9 %collective-permute-start.32 = (bf16[128,1024]{1,0:T(8,128)(2,1)S(1)}, bf16[128,1024]{1,0:T(8,128)(2,1)S(1)}, u32[]{:S(2)}, u32[]{:S(2)}) collective-permute-start(bf16[128,1024]{1,0:T(8,128)(2,1)S(1)} %bitcast.298), channel_id=1, source_target_pairs={} | collective-permute-start | bytes 786440 | tf_op jit(solution)/shard_map/ppermute | solution.py:25
  333.5 15.2 %collective-permute-start.25 = (bf16[128,1024]{1,0:T(8,128)(2,1)S(1)}, bf16[128,1024]{1,0:T(8,128)(2,1)S(1)}, u32[]{:S(2)}, u32[]{:S(2)}) collective-permute-start(bf16[128,1024]{1,0:T(8,128)(2,1)S(1)} %bitcast.297), channel_id=1, source_target_pairs={{2,0},{4,2},{6,4},{8,6},{10,8},{12,10},{14,12},{3,1},{5,3},{7,5},{... | collective-permute-start | bytes 786440 | tf_op jit(solution)/shard_map/ppermute | solution.py:25
Sparse Core Ops, SparseCore 0:
  10.8 54.6 all-gather.2
  67.1 17.2 all-gather.4
  331.2 111.4 all-reduce.3
where the time goes:
time: 457 us; the launch traced here: 452 us
  waiting for transfers between devices  221 us (48%)
  matrix products  83.4 us (18%)
  starting transfers between devices  76 us (17%)
  blocking collectives  23.9 us (5%)
  local copies, waits for them, and re-layouts  20.7 us (5%)
  between operations  14.4 us (3%)
  other arithmetic  13.1 us (3%)
    psum x1, waiting for transfers between devices, shards(): lax.psum((down_factor, up_factor), ('ctx', 'pair'))  91.6 us
    ppermute x32, waiting for transfers between devices, shifted(): return lax.ppermute(block, axis, route)  72.7 us
    ppermute x32, starting transfers between devices, shifted(): return lax.ppermute(block, axis, route)  70.4 us
    all_gather x1, waiting for transfers between devices, shards(): rows_half = lax.all_gather(own_half, 'ctx', axis=0, tiled=True)  56.3 us
    psum x1, blocking collectives, shards(): own_diff, counts = lax.psum((part_diff, part_count), 'ctx')  23.9 us
    dot_general x8, matrix products, per_head(): jnp.einsum('gtl,tgd->ld', weighted, grad_head, preferred_element_type=jnp...  22.8 us
    dot_general x8, matrix products, per_head(): jnp.einsum('gtl,ld->tgd', score_grad, key_head, preferred_element_type=jn...  14.9 us
    sub x8, matrix products, per_head(): weights_exp = jnp.where(allowed[None], jnp.exp(masked - row_max), 0.0)  13.8 us
  transfers between devices with their start and end apart: 36, of which 11 were waited for; matrix products, arithmetic and copies ran while one was open for 7% of the time, Pallas kernels for 0%

commit v1 on v0

v1 whole, which is shorter than its diff:
```python
import functools

import jax
import jax.numpy as jnp
from jax import lax
from jax.experimental import pallas as pl
from jax.experimental.pallas import tpu as pltpu
from jax.sharding import PartitionSpec as P

HEAD = 128
WINDOW = 1024
SEGS = 8
BETA = 0.1
LOSS = 256.0
ADAPT = 2.0
SCALE = 168.0**-0.5
NEG = -1e30
MESH = pl.DeviceIdType.MESH
F32 = jnp.float32
BF16 = jnp.bfloat16


def mm(a, b, ca, cb):
    return lax.dot_general(a, b, (((ca,), (cb,)), ((), ())), preferred_element_type=F32)


def kernel(
    n, L, D, NC, LOG,
    x_ref, q_ref, k_ref, w_ref, dn_ref, up_ref, g_ref, lab_ref, gap_ref,
    xg_ref, qg_ref, kg_ref, dd_ref, du_ref,
    wb, kb, vb, lb, sb, bias, lowr, pb, own, xr, zr, zs,
    hd, hu, rd, ru, crow,
    wring_s, wring_r, wpair_s, wpair_r,
    kz_s, kx_s, k_r, vz_s, vx_s, v_r, l_s, l_r, s_s, s_r,
    px_s, px_r, pz_s, pz_r, rd_s, rd_r, ru_s, ru_r,
):
    c = lax.axis_index("ctx")
    p = lax.axis_index("pair")
    even = lax.rem(c, 2) == 0
    odd = lax.rem(c, 2) == 1
    T = k_ref.shape[0]
    CW = k_ref.shape[1] // NC
    HALF = k_ref.shape[1] // 2

    def remote(src, dst, ss, rs, ctx, pair):
        return pltpu.make_async_remote_copy(
            src_ref=src, dst_ref=dst, send_sem=ss, recv_sem=rs,
            device_id={"ctx": ctx, "pair": pair}, device_id_type=MESH)

    barrier = pltpu.get_barrier_semaphore()
    me = c * 2 + p

    def greet(i, _):
        other = lax.rem(me + i, 2 * n)
        pl.semaphore_signal(barrier, inc=1, device_id={"ctx": other // 2, "pair": lax.rem(other, 2)},
                            device_id_type=MESH)
        return 0
    lax.fori_loop(1, 2 * n, greet, 0)
    pl.semaphore_wait(barrier, 2 * n - 1)

    pos = jnp.where(even, c // 2, n - 1 - c // 2)

    def at(position):
        r = lax.rem(position + 2 * n, n)
        return jnp.where(r < n // 2, 2 * r, 2 * (n - 1 - r) + 1)
    right, left = at(pos + 1), at(pos - 1)
    NR = n // 2
    NL = n - 1 - NR

    def hop(direction, slot, src, to):
        return remote(src, wb.at[slot, p], wring_s.at[direction, slot], wring_r.at[slot], to, p)

    def to_partner(slot):
        return remote(wb.at[slot, p], wb.at[slot, p], wpair_s.at[slot], wpair_r.at[slot], c, 1 - p)

    hop(0, c, w_ref.at[p], right).start()
    hop(1, c, w_ref.at[p], left).start()

    onehot = (lab_ref[...] == lax.broadcasted_iota(jnp.int32, (SEGS, T), 0).astype(F32)).astype(F32)
    part = jnp.sum(onehot * gap_ref[...], axis=1, keepdims=True)
    sb[p, c] = jnp.broadcast_to(part, (SEGS, 128))
    lb[0] = lab_ref[...]

    def sums(i):
        other = lax.rem(me + i, 2 * n)
        return remote(sb.at[p, c], sb.at[p, c], s_s.at[i], s_r.at[p, c], other // 2, lax.rem(other, 2))

    def send_sums(i, _):
        sums(i).start()
        return 0
    lax.fori_loop(1, 2 * n, send_sums, 0)

    def label(d):
        return remote(lb.at[0], lb.at[d], l_s.at[d], l_r.at[d], c + d, p)
    for d in range(1, D + 1):
        @pl.when(c + d < n)
        def _():
            label(d).start()

        @pl.when(c - d < 0)
        def _():
            kb[d] = jnp.zeros_like(kb[d])
            vb[d] = jnp.zeros_like(vb[d])
            lb[d] = jnp.full_like(lb[d], -1.0)

    def chain(buf, zs_, xs_, rs_, src, cols, ch):
        def cut(ref):
            return ref if cols is None else ref.at[:, cols]

        def z(k):
            return remote(cut(src if k == 0 else buf.at[2 * k]), cut(buf.at[2 * k + 2]), zs_.at[ch, k],
                          rs_.at[ch, 2 * k + 2], c + 2, p)

        def xe(k):
            return remote(cut(src if k == 0 else buf.at[2 * k]), cut(buf.at[2 * k + 1]), xs_.at[ch, k],
                          rs_.at[ch, 2 * k + 1], c + 1, p)

        def xo(k):
            return remote(cut(buf.at[2 * k]), cut(buf.at[2 * k - 1]), xs_.at[ch, k], rs_.at[ch, 2 * k - 1], c - 1, p)

        def each(k, do):
            if k < L:
                @pl.when((c + 2 < n) & (c - 2 * k >= 0))
                def _():
                    do(z(k))
            if 2 * k + 1 <= D:
                @pl.when(even & (c - 2 * k >= 0))
                def _():
                    do(xe(k))
            if k >= 1:
                @pl.when(odd & (c - 2 * k >= 0))
                def _():
                    do(xo(k))

        def arrived(d):
            @pl.when(c - d >= 0)
            def _():
                remote(cut(buf.at[d]), cut(buf.at[d]), zs_.at[ch, 0], rs_.at[ch, d], c - d, p).wait_recv()

        def step(k):
            if k >= 1:
                arrived(2 * k)
            each(k, lambda copy: copy.start())

        def rest():
            for d in range(1, D + 1, 2):
                arrived(d)

        def sent():
            for k in range(L + 1):
                each(k, lambda copy: copy.wait_send())
        return step, rest, sent

    k_step, k_rest, k_sent = chain(kb, kz_s, kx_s, k_r, k_ref, None, 0)
    k_step(0)
    kb[0] = k_ref[...]
    wb[c] = w_ref[...]

    def low_part(j, acc):
        return acc + mm(x_ref[j], dn_ref[j], 1, 0)
    lowr[...] = lax.fori_loop(0, n, low_part, jnp.zeros(lowr.shape, F32)).astype(BF16)

    def ring_step(s):
        slot = at(pos - s)
        hop(0, slot, wb.at[slot, p], right).wait_recv()

        @pl.when(s < NR)
        def _():
            hop(0, slot, wb.at[slot, p], right).start()
        to_partner(slot).start()

        @pl.when(s <= NL)
        def _():
            slot2 = at(pos + s)
            hop(1, slot2, wb.at[slot2, p], left).wait_recv()

            @pl.when(s < NL)
            def _():
                hop(1, slot2, wb.at[slot2, p], left).start()
            to_partner(slot2).start()

    if n <= 16:
        for s in range(1, NR + 1):
            ring_step(jnp.int32(s))
            if s <= L:
                k_step(s)
        for s in range(NR + 1, L + 1):
            k_step(s)
    else:
        def ring_body(s, _):
            ring_step(s)
            return 0
        lax.fori_loop(1, NR + 1, ring_body, 0)
        for s in range(1, L + 1):
            k_step(s)

    def partner_in(i, _):
        to_partner(lax.rem(c + i, n)).wait_recv()
        return 0
    lax.fori_loop(1, n, partner_in, 0)

    v_chains = []
    for ch in range(NC):
        lo = ch * CW
        cols = slice(lo, lo + CW)
        half, inner = lo // HALF, lo % HALF

        def value_part(j, acc):
            return acc + mm(x_ref[j], wb[j, half, :, inner:inner + CW], 1, 0)
        acc = lax.fori_loop(0, n, value_part, ADAPT * mm(lowr[...], up_ref[:, cols], 1, 0))
        vb[0, :, cols] = acc.astype(BF16)
        steps = chain(vb, vz_s, vx_s, v_r, vb.at[0], pl.ds(lo, CW), ch)
        v_chains.append(steps)
        steps[0](0)

    def sums_in(i, _):
        other = lax.rem(me + i, 2 * n)
        remote(sb.at[0, 0], sb.at[lax.rem(other, 2), other // 2], s_s.at[i], s_r.at[lax.rem(other, 2), other // 2],
               other // 2, lax.rem(other, 2)).wait_recv()
        return 0
    lax.fori_loop(1, 2 * n, sums_in, 0)
    margin = BETA * (jnp.sum(sb[0], axis=0) - jnp.sum(sb[1], axis=0))
    sign = 2.0 * p.astype(F32) - 1.0
    coef = sign * (BETA * LOSS) * jax.nn.sigmoid(-margin)
    token_coef = jnp.sum(onehot * coef, axis=0, keepdims=True)
    crow[...] = jnp.broadcast_to(jnp.concatenate([token_coef, token_coef], axis=1), crow.shape)

    lq = lab_ref[0:1, :]
    for d in range(D + 1):
        if d:
            @pl.when(c - d >= 0)
            def _():
                remote(lb.at[d], lb.at[d], l_s.at[d], l_r.at[d], c - d, p).wait_recv()
        lk = jnp.transpose(jnp.broadcast_to(lb[d][0:1, :], (T, T)))
        apart = (d * T + lax.broadcasted_iota(jnp.int32, (T, T), 1) - lax.broadcasted_iota(jnp.int32, (T, T), 0))
        ok = (lk == lq) & (apart >= 0) & (apart < WINDOW)
        b = jnp.where(ok, 0.0, NEG)
        bias[d * T:(d + 1) * T, :] = jnp.concatenate([b, b], axis=1)

    for k in range(1, L + 1):
        for ch in range(NC):
            v_chains[ch][0](k)
    k_rest()

    S = (D + 1) * T
    HC = CW // HEAD

    def px(ch, k, d, to):
        cs = pl.ds(ch * CW, CW)
        return remote(pb.at[d, :, :, cs], xr.at[k, :, :, cs], px_s.at[ch, k], px_r.at[ch, k], to, p)

    def parts_each(ch, do):
        for k in range(L + 1):
            if k >= 1:
                @pl.when(even & (c - 2 * k + 1 >= 0))
                def _():
                    do(px(ch, k, 2 * k - 1, c + 1))
            if 2 * k + 1 <= D:
                @pl.when(odd & (c - 2 * k - 1 >= 0))
                def _():
                    do(px(ch, k, 2 * k + 1, c - 1))

    def pz(ch, k):
        cs = pl.ds(ch * CW, CW)
        return remote(zs.at[k, :, :, cs], zr.at[k, :, :, cs], pz_s.at[ch, k], pz_r.at[ch, k], c - 2, p)

    def x_in(ch, k):
        px(ch, k, k, jnp.where(even, c + 1, c - 1)).wait_recv()

    def sum_chain(ch):
        cs = slice(ch * CW, (ch + 1) * CW)
        for k in range(L, -1, -1):
            @pl.when(c - 2 * k >= 0)
            def _():
                @pl.when(odd if 2 * k + 1 > D else (even if k == 0 else c >= 0))
                def _():
                    x_in(ch, k)
                if k + 1 <= L:
                    @pl.when(c + 2 < n)
                    def _():
                        pz(ch, k + 1).wait_recv()
                total = own[:, :, cs] if k == 0 else pb[2 * k, :, :, cs].astype(F32)
                use_x = odd if 2 * k + 1 > D else (even if k == 0 else c >= 0)
                total = total + jnp.where(use_x, xr[k, :, :, cs].astype(F32), 0.0)
                if k + 1 <= L:
                    total = total + jnp.where(c + 2 < n, zr[k + 1, :, :, cs].astype(F32), 0.0)
                if k == 0:
                    own[:, :, cs] = total
                else:
                    zs[k, :, :, cs] = total.astype(BF16)
                    pz(ch, k).start()

    for ch in range(NC):
        v_chains[ch][1]()

        def head(i, _):
            j = ch * HC + i
            hc = pl.ds(pl.multiple_of(j * HEAD, HEAD), HEAD)
            qa = pl.ds(pl.multiple_of(j * 2 * HEAD, HEAD), HEAD)
            qb = pl.ds(pl.multiple_of(j * 2 * HEAD + HEAD, HEAD), HEAD)
            qh = jnp.concatenate([q_ref[:, qa], q_ref[:, qb]], axis=0)
            gh = jnp.concatenate([g_ref[:, qa], g_ref[:, qb]], axis=0)
            kh = kb[:, :, hc].reshape(S, HEAD)
            vh = vb[:, :, hc].reshape(S, HEAD)
            cr = crow[0:1, :]
            s = mm(kh, qh, 1, 1) * SCALE + bias[...]
            e = jnp.exp(s - jnp.max(s, axis=0, keepdims=True))
            probs = e * (1.0 / jnp.sum(e, axis=0, keepdims=True))
            dp = mm(vh, gh, 1, 1) * cr
            delta = jnp.sum(probs * dp, axis=0, keepdims=True)
            ds = (SCALE * probs * (dp - delta)).astype(BF16)
            wt = (probs * cr).astype(BF16)
            dq = mm(ds, kh, 0, 0).astype(BF16)
            qg_ref[:, qa] = dq[:T]
            qg_ref[:, qb] = dq[T:]
            dk = mm(ds, qh, 1, 0)
            dv = mm(wt, gh, 1, 0)
            own[0, :, hc] = dk[:T]
            own[1, :, hc] = dv[:T]
            pb[1:, 0, :, hc] = dk[T:].astype(BF16).reshape(D, T, HEAD)
            pb[1:, 1, :, hc] = dv[T:].astype(BF16).reshape(D, T, HEAD)
            return 0
        lax.fori_loop(0, HC, head, 0)
        parts_each(ch, lambda copy: copy.start())
        if ch >= 1:
            sum_chain(ch - 1)
    sum_chain(NC - 1)

    kg_ref[...] = own[0].astype(BF16)
    vg = own[1].astype(BF16)
    mid = mm(vg, up_ref[...], 1, 1).astype(BF16)
    uf = ADAPT * mm(lowr[...], vg, 0, 0)
    for h in range(2):
        hu[h] = uf[:, h * HALF:(h + 1) * HALF]
    nh = n // 2

    def down_part(j, _):
        hd[j // nh, lax.rem(j, nh)] = ADAPT * mm(mid, x_ref[j], 0, 0)
        return 0
    lax.fori_loop(0, n, down_part, 0)

    def both(i, src, to, pair):
        return (remote(hd.at[src], rd.at[i], rd_s.at[i], rd_r.at[i], to, pair),
                remote(hu.at[src], ru.at[i], ru_s.at[i], ru_r.at[i], to, pair))

    def grad_part(j, _):
        g = mm(vg[:, :HALF], wb[j, 0], 1, 1) + mm(vg[:, HALF:], wb[j, 1], 1, 1)
        xg_ref[j] = (g + ADAPT * mm(mid, dn_ref[j], 1, 1)).astype(BF16)
        return 0

    rounds = LOG + 2
    for i in range(rounds):
        if i == 0:
            copies = both(i, 1 - p, c, 1 - p)
        elif i <= LOG:
            bit = 1 << (i - 1)
            to = jnp.where(lax.rem(c // bit, 2) == 0, c + bit, c - bit)
            copies = both(i, p, to, p)
        else:
            copies = both(i, p, c, 1 - p)
        for copy in copies:
            copy.start()
        lax.fori_loop(n * i // rounds, n * (i + 1) // rounds, grad_part, 0)
        for copy in copies:
            copy.wait()
        if i <= LOG:
            hd[p] = hd[p] + rd[i]
            hu[p] = hu[p] + ru[i]
    dd_ref[p] = hd[p]
    du_ref[p] = hu[p]
    dd_ref[1 - p] = rd[rounds - 1]
    du_ref[1 - p] = ru[rounds - 1]

    hop(0, c, w_ref.at[p], right).wait_send()
    hop(1, c, w_ref.at[p], left).wait_send()

    def ring_sent(s, _):
        slot = at(pos - s)

        @pl.when(s < NR)
        def _():
            hop(0, slot, wb.at[slot, p], right).wait_send()
        to_partner(slot).wait_send()

        @pl.when(s <= NL)
        def _():
            slot2 = at(pos + s)

            @pl.when(s < NL)
            def _():
                hop(1, slot2, wb.at[slot2, p], left).wait_send()
            to_partner(slot2).wait_send()
        return 0
    lax.fori_loop(1, NR + 1, ring_sent, 0)

    def sums_sent(i, _):
        sums(i).wait_send()
        return 0
    lax.fori_loop(1, 2 * n, sums_sent, 0)
    for d in range(1, D + 1):
        @pl.when(c + d < n)
        def _():
            label(d).wait_send()
    k_sent()
    for ch in range(NC):
        v_chains[ch][2]()
        parts_each(ch, lambda copy: copy.wait_send())
        for k in range(1, L + 1):
            @pl.when(c - 2 * k >= 0)
            def _():
                pz(ch, k).wait_send()


def shards(x, q, k, w, dn, up, g, plp, rlp, idx):
    n = lax.axis_size("ctx")
    T, width = k.shape[1], k.shape[2]
    rows = w.shape[0]
    R = -(-rows // 16) * 16
    model = x.shape[2]
    halo = WINDOW // T
    D = min(halo, n - 1)
    L = min(halo // 2, n // 2 - 1)
    NC = 4
    LOG = n.bit_length() - 1
    HALF = width // 2
    pad = R - rows
    xs = jnp.pad(x[0].reshape(T, n, rows).transpose(1, 0, 2), ((0, 0), (0, 0), (0, pad)))
    ws = jnp.pad(w.reshape(rows, 2, HALF).transpose(1, 0, 2), ((0, 0), (0, pad), (0, 0)))
    dns = jnp.pad(dn.reshape(n, rows, dn.shape[1]), ((0, 0), (0, pad), (0, 0)))
    lab = jnp.broadcast_to(idx.astype(F32), (SEGS, T))
    gap = jnp.broadcast_to(plp - rlp, (SEGS, T))
    rank = dn.shape[1]
    vm = pl.BlockSpec(memory_space=pltpu.VMEM)
    dma = pltpu.SemaphoreType.DMA
    xg, qg, kg, dd, du = pl.pallas_call(
        functools.partial(kernel, n, L, D, NC, LOG),
        out_shape=(
            jax.ShapeDtypeStruct((n, T, R), BF16),
            jax.ShapeDtypeStruct(q.shape[1:], BF16),
            jax.ShapeDtypeStruct(k.shape[1:], BF16),
            jax.ShapeDtypeStruct((2, n // 2, rank, R), F32),
            jax.ShapeDtypeStruct((2, rank, HALF), F32),
        ),
        in_specs=[vm] * 9,
        out_specs=[vm] * 5,
        scratch_shapes=[
            pltpu.VMEM((n, 2, R, HALF), BF16),
            pltpu.VMEM((D + 1, T, width), BF16),
            pltpu.VMEM((D + 1, T, width), BF16),
            pltpu.VMEM((D + 1, SEGS, T), F32),
            pltpu.VMEM((2, n, SEGS, 128), F32),
            pltpu.VMEM(((D + 1) * T, 2 * T), F32),
            pltpu.VMEM((T, rank), BF16),
            pltpu.VMEM((D + 1, 2, T, width), BF16),
            pltpu.VMEM((2, T, width), F32),
            pltpu.VMEM((L + 1, 2, T, width), BF16),
            pltpu.VMEM((L + 1, 2, T, width), BF16),
            pltpu.VMEM((L + 1, 2, T, width), BF16),
            pltpu.VMEM((2, n // 2, rank, R), F32),
            pltpu.VMEM((2, rank, HALF), F32),
            pltpu.VMEM((LOG + 2, n // 2, rank, R), F32),
            pltpu.VMEM((LOG + 2, rank, HALF), F32),
            pltpu.VMEM((8, 2 * T), F32),
            dma((2, n)), dma((n,)), dma((n,)), dma((n,)),
            dma((1, L + 1)), dma((1, L + 1)), dma((1, D + 1)),
            dma((NC, L + 1)), dma((NC, L + 1)), dma((NC, D + 1)),
            dma((D + 1,)), dma((D + 1,)), dma((2 * n,)), dma((2, n)),
            dma((NC, L + 1)), dma((NC, L + 1)), dma((NC, L + 1)), dma((NC, L + 1)),
            dma((LOG + 2,)), dma((LOG + 2,)), dma((LOG + 2,)), dma((LOG + 2,)),
        ],
        compiler_params=pltpu.CompilerParams(
            collective_id=0, has_side_effects=True, vmem_limit_bytes=60 * 1024 * 1024),
    )(xs, q[0], k[0], ws, dns, up, g[0], lab, gap)
    input_grad = xg[:, :, :rows].transpose(1, 0, 2).reshape(T, model)
    down = dd.reshape(n, rank, R)[:, :, :rows].transpose(0, 2, 1).reshape(model, rank)
    upg = du.transpose(1, 0, 2).reshape(rank, width)
    return input_grad[None], qg[None], kg[None], down, upg


def solution(mesh):
    tok = P(("grp", "pair"), "ctx", None)
    row = P(("grp", "pair"), "ctx")
    return jax.shard_map(
        shards,
        mesh=mesh,
        in_specs=(tok, tok, tok, P("ctx", None), P(), P(), tok, row, row, row),
        out_specs=(tok, tok, tok, P("grp", None), P("grp", None)),
        check_vma=False,
    )
```

time: 457 us -> 181 us (0.40)
  waiting for transfers between devices: 221 us -> 0 us
  Pallas kernels: 0 us -> 167 us
  matrix products: 83.4 us -> 0 us
  starting transfers between devices: 76 us -> 0 us
  blocking collectives: 23.9 us -> 0 us
  between operations: 14.4 us -> 0.7 us
  other arithmetic: 13.1 us -> 0.01 us
  local copies, waits for them, and re-layouts: 20.7 us -> 13.1 us
    pallas_call x0 -> x1, Pallas kernels: none -> 167 us  [shards(): pl.pallas_call(functools.partial(kernel, n, L, D, NC, LOG), out_shape=(ja...]
    psum x1 -> x0, waiting for transfers between devices: 91.6 us -> none  [shards(): lax.psum((down_factor, up_factor), ('ctx', 'pair'))]
    ppermute x33 -> x0, starting transfers between devices: 75.9 us -> none  [the longest x32 70.4 us: shifted(): return lax.ppermute(block, axis, route)]
    ppermute x33 -> x0, waiting for transfers between devices: 72.7 us -> none  [the longest x32 72.7 us: shifted(): return lax.ppermute(block, axis, route)]
    dot_general x40 -> x0, matrix products: 69.6 us -> none  [the longest x8 22.8 us: per_head(): jnp.einsum('gtl,tgd->ld', weighted, grad_head, preferred_element_type=jnp...]
    all_gather x2 -> x0, waiting for transfers between devices: 56.3 us -> none  [the longest x1 56.3 us: shards(): rows_half = lax.all_gather(own_half, 'ctx', axis=0, tiled=True)]
    psum x1 -> x0, blocking collectives: 23.9 us -> none  [shards(): own_diff, counts = lax.psum((part_diff, part_count), 'ctx')]
    sub x8 -> x0, matrix products: 13.8 us -> none  [per_head(): weights_exp = jnp.where(allowed[None], jnp.exp(masked - row_max), 0.0)]
  transfers between devices with their start and end apart: 36 -> 0, of which waited for: 11 -> 0; matrix products, arithmetic and copies ran while one was open for 7% -> 0% of each run, Pallas kernels for 0% -> 0%
where the time goes in v1:
time: 181 us
  Pallas kernels  167 us (92%)
  local copies, waits for them, and re-layouts  13.1 us (7%)
    pallas_call x1, Pallas kernels, shards(): pl.pallas_call(functools.partial(kernel, n, L, D, NC, LOG), out_shape=(ja...  167 us
    unnamed x23, local copies, waits for them, and re-layouts  6.85 us

profile of v1, /device:TPU:27, one launch (start us, length us, event | category | flops | bytes accessed | tf_op | source)
XLA Modules:
  0.0 180.7 jit_solution(5879250185772496399)
XLA Ops:
  0.6 0.0 copy-start.6
  0.6 0.0 copy-start.7
  0.7 0.6 copy-done.6
  1.3 0.0 copy-done.7
  1.3 0.0 copy-start.8
  1.3 0.6 copy-done.8
  2.0 0.6 broadcast_in_dim.21.lab_ref
  2.6 0.6 broadcast_in_dim.23.gap_ref
  3.2 1.4 copy.17
  4.6 0.0 copy-start
  4.6 1.2 copy.18
  5.8 0.0 copy-done
  5.8 0.0 copy-start.4
  5.8 0.9 copy.28
  6.7 0.0 copy-done.4
  6.7 1.2 copy.20
  7.8 166.9 %shard_map.137 = (bf16[8,128,336]{2,1,0:T(8,128)(2,1)}, bf16[128,2048]{1,0:T(8,128)(2,1)}, bf16[128,1024]{1,0:T(8,128)(2,1)}, f32[2,4,16,336]{3,2,1,0:T(8,128)}, f32[2,16,512]{2,1,0:T(8,128)}) custom-call(bf16[8,128,336]{2,1,0:T(8,128)(2,1)} %bitcast.29, bf16[128,2048]{1,0:T(8,128)(2,1)} %bitcast.37, bf16[128,1024]{1,0:T(8,128)(2,1)} %bitcast.40, ...), custom_call_target="tpu_custom_call" | custom-call | tf_op jit(solution)/shard_map/pallas_call | solution.py:435
  174.8 1.5 copy.21
  176.3 0.0 copy-start.5
  176.3 0.0 copy-start.3
  176.3 1.1 copy.24
  177.4 0.0 copy-start.1
  177.4 0.0 copy-done.5
  177.4 0.6 copy.26
  178.0 0.0 copy-done.3
  178.0 0.1 copy.22
  178.1 0.8 reshape.28
  178.9 0.0 copy-done.1
  178.9 0.0 copy-start.2
  178.9 0.8 copy.31
  179.7 0.3 copy-done.2
  180.0 0.7 copy.32
  (2 shorter events, 0.0 us)
Async XLA Ops:
  0.6 0.7 copy-start.6
  0.6 0.7 copy-start.7
  1.3 0.7 copy-start.8
  4.6 1.2 copy-start
  5.8 0.9 copy-start.4
  176.3 1.2 copy-start.5
  176.3 1.8 copy-start.3
  177.4 1.5 copy-start.1
  178.9 1.1 copy-start.2

commit v2 on v1

--- a/solution.py
+++ b/solution.py
@@ -29,7 +29,7 @@
     x_ref, q_ref, k_ref, w_ref, dn_ref, up_ref, g_ref, lab_ref, gap_ref,
     xg_ref, qg_ref, kg_ref, dd_ref, du_ref,
     wb, kb, vb, lb, sb, bias, lowr, pb, own, xr, zr, zs,
-    hd, hu, rd, ru, crow,
+    hd, hu, hdb, hub, rd, ru, rfd, rfu, crow,
     wring_s, wring_r, wpair_s, wpair_r,
     kz_s, kx_s, k_r, vz_s, vx_s, v_r, l_s, l_r, s_s, s_r,
     px_s, px_r, pz_s, pz_r, rd_s, rd_r, ru_s, ru_r,
@@ -41,6 +41,11 @@
     T = k_ref.shape[0]
     CW = k_ref.shape[1] // NC
     HALF = k_ref.shape[1] // 2
+    M = x_ref.shape[1]
+    R = M // n
+
+    def block(slot):
+        return wb.at[p, pl.ds(pl.multiple_of(slot * R, 16), R), :]
 
     def remote(src, dst, ss, rs, ctx, pair):
         return pltpu.make_async_remote_copy(
@@ -68,10 +73,10 @@
     NL = n - 1 - NR
 
     def hop(direction, slot, src, to):
-        return remote(src, wb.at[slot, p], wring_s.at[direction, slot], wring_r.at[slot], to, p)
+        return remote(src, block(slot), wring_s.at[direction, slot], wring_r.at[slot], to, p)
 
     def to_partner(slot):
-        return remote(wb.at[slot, p], wb.at[slot, p], wpair_s.at[slot], wpair_r.at[slot], c, 1 - p)
+        return remote(block(slot), block(slot), wpair_s.at[slot], wpair_r.at[slot], c, 1 - p)
 
     hop(0, c, w_ref.at[p], right).start()
     hop(1, c, w_ref.at[p], left).start()
@@ -154,29 +159,28 @@
     k_step, k_rest, k_sent = chain(kb, kz_s, kx_s, k_r, k_ref, None, 0)
     k_step(0)
     kb[0] = k_ref[...]
-    wb[c] = w_ref[...]
-
-    def low_part(j, acc):
-        return acc + mm(x_ref[j], dn_ref[j], 1, 0)
-    lowr[...] = lax.fori_loop(0, n, low_part, jnp.zeros(lowr.shape, F32)).astype(BF16)
+    for h in range(2):
+        wb[h, pl.ds(pl.multiple_of(c * R, 16), R), :] = w_ref[h]
+
+    lowr[...] = mm(x_ref[...], dn_ref[...], 1, 0).astype(BF16)
 
     def ring_step(s):
         slot = at(pos - s)
-        hop(0, slot, wb.at[slot, p], right).wait_recv()
+        hop(0, slot, block(slot), right).wait_recv()
 
         @pl.when(s < NR)
         def _():
-            hop(0, slot, wb.at[slot, p], right).start()
+            hop(0, slot, block(slot), right).start()
         to_partner(slot).start()
 
         @pl.when(s <= NL)
         def _():
             slot2 = at(pos + s)
-            hop(1, slot2, wb.at[slot2, p], left).wait_recv()
+            hop(1, slot2, block(slot2), left).wait_recv()
 
             @pl.when(s < NL)
             def _():
-                hop(1, slot2, wb.at[slot2, p], left).start()
+                hop(1, slot2, block(slot2), left).start()
             to_partner(slot2).start()
 
     if n <= 16:
@@ -205,9 +209,7 @@
         cols = slice(lo, lo + CW)
         half, inner = lo // HALF, lo % HALF
 
-        def value_part(j, acc):
-            return acc + mm(x_ref[j], wb[j, half, :, inner:inner + CW], 1, 0)
-        acc = lax.fori_loop(0, n, value_part, ADAPT * mm(lowr[...], up_ref[:, cols], 1, 0))
+        acc = mm(x_ref[...], wb[half, :, inner:inner + CW], 1, 0) + ADAPT * mm(lowr[...], up_ref[:, cols], 1, 0)
         vb[0, :, cols] = acc.astype(BF16)
         steps = chain(vb, vz_s, vx_s, v_r, vb.at[0], pl.ds(lo, CW), ch)
         v_chains.append(steps)
@@ -237,9 +239,11 @@
         b = jnp.where(ok, 0.0, NEG)
         bias[d * T:(d + 1) * T, :] = jnp.concatenate([b, b], axis=1)
 
-    for k in range(1, L + 1):
-        for ch in range(NC):
+    def values_up(ch):
+        for k in range(1, L + 1):
             v_chains[ch][0](k)
+
+    values_up(0)
     k_rest()
 
     S = (D + 1) * T
@@ -250,7 +254,7 @@
         return remote(pb.at[d, :, :, cs], xr.at[k, :, :, cs], px_s.at[ch, k], px_r.at[ch, k], to, p)
 
     def parts_each(ch, do):
-        for k in range(L + 1):
+        for k in range(L, -1, -1):
             if k >= 1:
                 @pl.when(even & (c - 2 * k + 1 >= 0))
                 def _():
@@ -291,6 +295,8 @@
                     pz(ch, k).start()
 
     for ch in range(NC):
+        if ch + 1 < NC:
+            values_up(ch + 1)
         v_chains[ch][1]()
 
         def head(i, _):
@@ -332,44 +338,51 @@
     uf = ADAPT * mm(lowr[...], vg, 0, 0)
     for h in range(2):
         hu[h] = uf[:, h * HALF:(h + 1) * HALF]
-    nh = n // 2
-
-    def down_part(j, _):
-        hd[j // nh, lax.rem(j, nh)] = ADAPT * mm(mid, x_ref[j], 0, 0)
-        return 0
-    lax.fori_loop(0, n, down_part, 0)
-
-    def both(i, src, to, pair):
-        return (remote(hd.at[src], rd.at[i], rd_s.at[i], rd_r.at[i], to, pair),
-                remote(hu.at[src], ru.at[i], ru_s.at[i], ru_r.at[i], to, pair))
+    df = ADAPT * mm(mid, x_ref[...], 0, 0)
+    for h in range(2):
+        hd[h] = df[:, h * (M // 2):(h + 1) * (M // 2)]
+
+    def both(i, src_d, src_u, dst_d, dst_u, to, pair):
+        return (remote(src_d, dst_d, rd_s.at[i], rd_r.at[i], to, pair),
+                remote(src_u, dst_u, ru_s.at[i], ru_r.at[i], to, pair))
+
+    tile = 384 if M % 384 == 0 else 128
 
     def grad_part(j, _):
-        g = mm(vg[:, :HALF], wb[j, 0], 1, 1) + mm(vg[:, HALF:], wb[j, 1], 1, 1)
-        xg_ref[j] = (g + ADAPT * mm(mid, dn_ref[j], 1, 1)).astype(BF16)
+        t = pl.ds(pl.multiple_of(j * tile, tile), tile)
+        g = mm(vg[:, :HALF], wb[0, t, :], 1, 1) + mm(vg[:, HALF:], wb[1, t, :], 1, 1)
+        xg_ref[:, t] = (g + ADAPT * mm(mid, dn_ref[t, :], 1, 1)).astype(BF16)
         return 0
 
     rounds = LOG + 2
+    tiles = M // tile
     for i in range(rounds):
-        if i == 0:
-            copies = both(i, 1 - p, c, 1 - p)
-        elif i <= LOG:
-            bit = 1 << (i - 1)
-            to = jnp.where(lax.rem(c // bit, 2) == 0, c + bit, c - bit)
-            copies = both(i, p, to, p)
+        if i <= LOG:
+            at_half = 1 - p if i == 0 else p
+            hdb[...] = hd[at_half].astype(BF16)
+            hub[...] = hu[at_half].astype(BF16)
+            if i == 0:
+                to, pair = c, 1 - p
+            else:
+                bit = 1 << (i - 1)
+                to, pair = jnp.where(lax.rem(c // bit, 2) == 0, c + bit, c - bit), p
+            copies = both(i, hdb, hub, rd.at[i], ru.at[i], to, pair)
         else:
-            copies = both(i, p, c, 1 - p)
+            copies = both(i, hd.at[p], hu.at[p], rfd, rfu, c, 1 - p)
         for copy in copies:
             copy.start()
-        lax.fori_loop(n * i // rounds, n * (i + 1) // rounds, grad_part, 0)
+        lax.fori_loop(tiles * i // rounds, tiles * (i + 1) // rounds, grad_part, 0)
         for copy in copies:
             copy.wait()
         if i <= LOG:
-            hd[p] = hd[p] + rd[i]
-            hu[p] = hu[p] + ru[i]
+            mine_d = hd[p] if i == 0 else hdb[...].astype(F32)
+            mine_u = hu[p] if i == 0 else hub[...].astype(F32)
+            hd[p] = mine_d + rd[i].astype(F32)
+            hu[p] = mine_u + ru[i].astype(F32)
     dd_ref[p] = hd[p]
     du_ref[p] = hu[p]
-    dd_ref[1 - p] = rd[rounds - 1]
-    du_ref[1 - p] = ru[rounds - 1]
+    dd_ref[1 - p] = rfd[...]
+    du_ref[1 - p] = rfu[...]
 
     hop(0, c, w_ref.at[p], right).wait_send()
     hop(1, c, w_ref.at[p], left).wait_send()
@@ -379,7 +392,7 @@
 
         @pl.when(s < NR)
         def _():
-            hop(0, slot, wb.at[slot, p], right).wait_send()
+            hop(0, slot, block(slot), right).wait_send()
         to_partner(slot).wait_send()
 
         @pl.when(s <= NL)
@@ -388,7 +401,7 @@
 
             @pl.when(s < NL)
             def _():
-                hop(1, slot2, wb.at[slot2, p], left).wait_send()
+                hop(1, slot2, block(slot2), left).wait_send()
             to_partner(slot2).wait_send()
         return 0
     lax.fori_loop(1, NR + 1, ring_sent, 0)
@@ -424,9 +437,14 @@
     LOG = n.bit_length() - 1
     HALF = width // 2
     pad = R - rows
-    xs = jnp.pad(x[0].reshape(T, n, rows).transpose(1, 0, 2), ((0, 0), (0, 0), (0, pad)))
+    M = n * R
+    xs = x[0]
+    if pad:
+        xs = jnp.pad(xs.reshape(T, n, rows), ((0, 0), (0, 0), (0, pad))).reshape(T, M)
     ws = jnp.pad(w.reshape(rows, 2, HALF).transpose(1, 0, 2), ((0, 0), (0, pad), (0, 0)))
-    dns = jnp.pad(dn.reshape(n, rows, dn.shape[1]), ((0, 0), (0, pad), (0, 0)))
+    dns = dn
+    if pad:
+        dns = jnp.pad(dn.reshape(n, rows, dn.shape[1]), ((0, 0), (0, pad), (0, 0))).reshape(M, dn.shape[1])
     lab = jnp.broadcast_to(idx.astype(F32), (SEGS, T))
     gap = jnp.broadcast_to(plp - rlp, (SEGS, T))
     rank = dn.shape[1]
@@ -435,16 +453,16 @@
     xg, qg, kg, dd, du = pl.pallas_call(
         functools.partial(kernel, n, L, D, NC, LOG),
         out_shape=(
-            jax.ShapeDtypeStruct((n, T, R), BF16),
+            jax.ShapeDtypeStruct((T, M), BF16),
             jax.ShapeDtypeStruct(q.shape[1:], BF16),
             jax.ShapeDtypeStruct(k.shape[1:], BF16),
-            jax.ShapeDtypeStruct((2, n // 2, rank, R), F32),
+            jax.ShapeDtypeStruct((2, rank, M // 2), F32),
             jax.ShapeDtypeStruct((2, rank, HALF), F32),
         ),
         in_specs=[vm] * 9,
         out_specs=[vm] * 5,
         scratch_shapes=[
-            pltpu.VMEM((n, 2, R, HALF), BF16),
+            pltpu.VMEM((2, M, HALF), BF16),
             pltpu.VMEM((D + 1, T, width), BF16),
             pltpu.VMEM((D + 1, T, width), BF16),
             pltpu.VMEM((D + 1, SEGS, T), F32),
@@ -456,10 +474,14 @@
             pltpu.VMEM((L + 1, 2, T, width), BF16),
             pltpu.VMEM((L + 1, 2, T, width), BF16),
             pltpu.VMEM((L + 1, 2, T, width), BF16),
-            pltpu.VMEM((2, n // 2, rank, R), F32),
+            pltpu.VMEM((2, rank, M // 2), F32),
             pltpu.VMEM((2, rank, HALF), F32),
-            pltpu.VMEM((LOG + 2, n // 2, rank, R), F32),
-            pltpu.VMEM((LOG + 2, rank, HALF), F32),
+            pltpu.VMEM((rank, M // 2), BF16),
+            pltpu.VMEM((rank, HALF), BF16),
+            pltpu.VMEM((LOG + 1, rank, M // 2), BF16),
+            pltpu.VMEM((LOG + 1, rank, HALF), BF16),
+            pltpu.VMEM((rank, M // 2), F32),
+            pltpu.VMEM((rank, HALF), F32),
             pltpu.VMEM((8, 2 * T), F32),
             dma((2, n)), dma((n,)), dma((n,)), dma((n,)),
             dma((1, L + 1)), dma((1, L + 1)), dma((1, D + 1)),
@@ -471,8 +493,11 @@
         compiler_params=pltpu.CompilerParams(
             collective_id=0, has_side_effects=True, vmem_limit_bytes=60 * 1024 * 1024),
     )(xs, q[0], k[0], ws, dns, up, g[0], lab, gap)
-    input_grad = xg[:, :, :rows].transpose(1, 0, 2).reshape(T, model)
-    down = dd.reshape(n, rank, R)[:, :, :rows].transpose(0, 2, 1).reshape(model, rank)
+    input_grad = xg
+    down = dd.transpose(0, 2, 1).reshape(M, rank)
+    if pad:
+        input_grad = xg.reshape(T, n, R)[:, :, :rows].reshape(T, model)
+        down = down.reshape(n, R, rank)[:, :rows].reshape(model, rank)
     upg = du.transpose(1, 0, 2).reshape(rank, width)
     return input_grad[None], qg[None], kg[None], down, upg
 

time: 181 us -> 162 us (0.90)
  Pallas kernels: 167 us -> 149 us
    pallas_call x1, Pallas kernels: 167 us -> 149 us  [shards(): pl.pallas_call(functools.partial(kernel, n, L, D, NC, LOG), out_shape=(ja...]
    unnamed x23 -> x18, local copies, waits for them, and re-layouts: 6.85 us -> 5.52 us
where the time goes in v2:
time: 162 us
  Pallas kernels  149 us (92%)
  local copies, waits for them, and re-layouts  12.1 us (7%)
    pallas_call x1, Pallas kernels, shards(): pl.pallas_call(functools.partial(kernel, n, L, D, NC, LOG), out_shape=(ja...  149 us
    unnamed x18, local copies, waits for them, and re-layouts  5.52 us

profile of v2, /device:TPU:27, one launch (start us, length us, event | category | flops | bytes accessed | tf_op | source)
XLA Modules:
  0.0 162.0 jit_solution(452291754776574991)
XLA Ops:
  0.6 0.0 copy-start.4
  0.6 0.0 copy-start.5
  0.7 0.6 copy-done.4
  1.3 0.0 copy-done.5
  1.3 0.0 copy-start.6
  1.3 0.6 copy-done.6
  2.0 0.6 broadcast_in_dim.24.lab_ref
  2.6 0.6 broadcast_in_dim.26.gap_ref
  3.2 0.0 copy-start.3
  3.2 2.0 %copy.23 = bf16[42,2,8,512]{3,2,0,1:T(8,128)(2,1)} copy(bf16[42,2,8,512]{3,2,1,0:T(8,128)(2,1)} %bitcast.25) | data formatting | bytes 1376256 | tf_op jit(solution)/shard_map/reshape | solution.py:444
  5.2 0.0 copy-done.3
  5.2 1.1 copy.17.dn_ref
  6.3 149.2 %shard_map.137 = (bf16[128,2688]{1,0:T(8,128)(2,1)}, bf16[128,2048]{1,0:T(8,128)(2,1)}, bf16[128,1024]{1,0:T(8,128)(2,1)}, f32[2,16,1344]{2,1,0:T(8,128)}, f32[2,16,512]{2,1,0:T(8,128)}) custom-call(bf16[128,2688]{1,0:T(8,128)(2,1)} %bitcast.26, bf16[128,2048]{1,0:T(8,128)(2,1)} %bitcast.29, bf16[128,1024]{1,0:T(8,128)(2,1)} %bitcast.32, ...), custom_call_target="tpu_custom_call" | custom-call | tf_op jit(solution)/shard_map/pallas_call | solution.py:453
  155.5 0.0 copy-start
  155.5 1.5 copy.21
  157.0 1.0 copy.18
  158.0 0.8 reshape.20
  158.9 0.0 copy-done
  158.9 0.0 copy-start.1
  158.9 0.8 copy.27
  159.7 0.4 copy-done.1
  160.2 0.0 copy-start.2
  160.2 0.8 copy.28
  161.0 0.3 copy-done.2
  161.3 0.7 copy.29
  (2 shorter events, 0.0 us)
Async XLA Ops:
  0.6 0.7 copy-start.4
  0.6 0.7 copy-start.5
  1.3 0.7 copy-start.6
  3.2 2.0 %copy-start.3 = (bf16[2688,16]{0,1:T(8,128)(2,1)S(1)}, bf16[2688,16]{0,1:T(8,128)(2,1)}, u32[]{:S(2)}) copy-start(bf16[2688,16]{0,1:T(8,128)(2,1)} %param.14) | copy-start | bytes 258052
  155.5 3.4 %copy-start = (bf16[128,2688]{1,0:T(8,128)(2,1)S(1)}, bf16[128,2688]{1,0:T(8,128)(2,1)}, u32[]{:S(2)}) copy-start(bf16[128,2688]{1,0:T(8,128)(2,1)} %get-tuple-element.10) | copy-start | bytes 2064388
  158.9 1.3 copy-start.1
  160.2 1.1 copy-start.2

commit v3 on v2

--- a/solution.py
+++ b/solution.py
@@ -30,7 +30,7 @@
     xg_ref, qg_ref, kg_ref, dd_ref, du_ref,
     wb, kb, vb, lb, sb, bias, lowr, pb, own, xr, zr, zs,
     hd, hu, hdb, hub, rd, ru, rfd, rfu, crow,
-    wring_s, wring_r, wpair_s, wpair_r,
+    wring_s, wring_r, wpair_s, wpair_r, wy_s, wy_r, wrest_s, wrest_r,
     kz_s, kx_s, k_r, vz_s, vx_s, v_r, l_s, l_r, s_s, s_r,
     px_s, px_r, pz_s, pz_r, rd_s, rd_r, ru_s, ru_r,
 ):
@@ -44,8 +44,28 @@
     M = x_ref.shape[1]
     R = M // n
 
+    y = lax.axis_index("grp")
+    U = R * 2 // 7 // 16 * 16
+
     def block(slot):
-        return wb.at[p, pl.ds(pl.multiple_of(slot * R, 16), R), :]
+        return wb.at[p, pl.ds(pl.multiple_of(slot * R + y * U, 16), R - U), :]
+
+    def across(slot, mine):
+        first = (y if mine else 1 - y) * (R - U)
+        return wb.at[p, pl.ds(pl.multiple_of(slot * R + first, 16), U), :]
+
+    def to_group(slot):
+        return pltpu.make_async_remote_copy(
+            src_ref=across(slot, True), dst_ref=across(slot, True), send_sem=wy_s.at[slot], recv_sem=wy_r.at[slot],
+            device_id={"grp": 1 - y, "ctx": c, "pair": p}, device_id_type=MESH)
+
+    def group_in(slot):
+        return pltpu.make_async_remote_copy(
+            src_ref=across(slot, False), dst_ref=across(slot, False), send_sem=wy_s.at[slot], recv_sem=wy_r.at[slot],
+            device_id={"grp": 1 - y, "ctx": c, "pair": p}, device_id_type=MESH)
+
+    def rest_to_partner(slot):
+        return remote(across(slot, False), across(slot, False), wrest_s.at[slot], wrest_r.at[slot], c, 1 - p)
 
     def remote(src, dst, ss, rs, ctx, pair):
         return pltpu.make_async_remote_copy(
@@ -61,7 +81,9 @@
                             device_id_type=MESH)
         return 0
     lax.fori_loop(1, 2 * n, greet, 0)
-    pl.semaphore_wait(barrier, 2 * n - 1)
+    if U:
+        pl.semaphore_signal(barrier, inc=1, device_id={"grp": 1 - y, "ctx": c, "pair": p}, device_id_type=MESH)
+    pl.semaphore_wait(barrier, 2 * n if U else 2 * n - 1)
 
     pos = jnp.where(even, c // 2, n - 1 - c // 2)
 
@@ -78,8 +100,8 @@
     def to_partner(slot):
         return remote(block(slot), block(slot), wpair_s.at[slot], wpair_r.at[slot], c, 1 - p)
 
-    hop(0, c, w_ref.at[p], right).start()
-    hop(1, c, w_ref.at[p], left).start()
+    hop(0, c, w_ref.at[p, pl.ds(pl.multiple_of(y * U, 16), R - U), :], right).start()
+    hop(1, c, w_ref.at[p, pl.ds(pl.multiple_of(y * U, 16), R - U), :], left).start()
 
     onehot = (lab_ref[...] == lax.broadcasted_iota(jnp.int32, (SEGS, T), 0).astype(F32)).astype(F32)
     part = jnp.sum(onehot * gap_ref[...], axis=1, keepdims=True)
@@ -172,6 +194,8 @@
         def _():
             hop(0, slot, block(slot), right).start()
         to_partner(slot).start()
+        if U:
+            to_group(slot).start()
 
         @pl.when(s <= NL)
         def _():
@@ -182,6 +206,8 @@
             def _():
                 hop(1, slot2, block(slot2), left).start()
             to_partner(slot2).start()
+            if U:
+                to_group(slot2).start()
 
     if n <= 16:
         for s in range(1, NR + 1):
@@ -198,8 +224,33 @@
         for s in range(1, L + 1):
             k_step(s)
 
+    if U:
+        def group_arrived(s, _):
+            slot = at(pos - s)
+            group_in(slot).wait_recv()
+            rest_to_partner(slot).start()
+
+            @pl.when(s <= NL)
+            def _():
+                slot2 = at(pos + s)
+                group_in(slot2).wait_recv()
+                rest_to_partner(slot2).start()
+            return 0
+        lax.fori_loop(1, NR + 1, group_arrived, 0)
+
+    def partner_rows(slot):
+        return wb.at[1 - p, pl.ds(pl.multiple_of(slot * R + y * U, 16), R - U), :]
+
+    def partner_rest(slot):
+        return wb.at[1 - p, pl.ds(pl.multiple_of(slot * R + (1 - y) * (R - U), 16), U), :]
+
     def partner_in(i, _):
-        to_partner(lax.rem(c + i, n)).wait_recv()
+        slot = lax.rem(c + i, n)
+        rows = partner_rows(slot)
+        remote(rows, rows, wpair_s.at[slot], wpair_r.at[slot], c, 1 - p).wait_recv()
+        if U:
+            more = partner_rest(slot)
+            remote(more, more, wrest_s.at[slot], wrest_r.at[slot], c, 1 - p).wait_recv()
         return 0
     lax.fori_loop(1, n, partner_in, 0)
 
@@ -384,8 +435,8 @@
     dd_ref[1 - p] = rfd[...]
     du_ref[1 - p] = rfu[...]
 
-    hop(0, c, w_ref.at[p], right).wait_send()
-    hop(1, c, w_ref.at[p], left).wait_send()
+    hop(0, c, w_ref.at[p, pl.ds(pl.multiple_of(y * U, 16), R - U), :], right).wait_send()
+    hop(1, c, w_ref.at[p, pl.ds(pl.multiple_of(y * U, 16), R - U), :], left).wait_send()
 
     def ring_sent(s, _):
         slot = at(pos - s)
@@ -394,6 +445,9 @@
         def _():
             hop(0, slot, block(slot), right).wait_send()
         to_partner(slot).wait_send()
+        if U:
+            to_group(slot).wait_send()
+            rest_to_partner(slot).wait_send()
 
         @pl.when(s <= NL)
         def _():
@@ -403,6 +457,9 @@
             def _():
                 hop(1, slot2, block(slot2), left).wait_send()
             to_partner(slot2).wait_send()
+            if U:
+                to_group(slot2).wait_send()
+                rest_to_partner(slot2).wait_send()
         return 0
     lax.fori_loop(1, NR + 1, ring_sent, 0)
 
@@ -483,7 +540,7 @@
             pltpu.VMEM((rank, M // 2), F32),
             pltpu.VMEM((rank, HALF), F32),
             pltpu.VMEM((8, 2 * T), F32),
-            dma((2, n)), dma((n,)), dma((n,)), dma((n,)),
+            dma((2, n)), dma((n,)), dma((n,)), dma((n,)), dma((n,)), dma((n,)), dma((n,)), dma((n,)),
             dma((1, L + 1)), dma((1, L + 1)), dma((1, D + 1)),
             dma((NC, L + 1)), dma((NC, L + 1)), dma((NC, D + 1)),
             dma((D + 1,)), dma((D + 1,)), dma((2 * n,)), dma((2, n)),

time: 162 us -> 157 us (0.969)
  Pallas kernels: 149 us -> 144 us
    pallas_call x1, Pallas kernels: 149 us -> 144 us  [shards(): pl.pallas_call(functools.partial(kernel, n, L, D, NC, LOG), out_shape=(ja...]
where the time goes in v3:
time: 157 us; the launch traced here: 156 us
  Pallas kernels  144 us (92%)
  local copies, waits for them, and re-layouts  12.1 us (8%)
    pallas_call x1, Pallas kernels, shards(): pl.pallas_call(functools.partial(kernel, n, L, D, NC, LOG), out_shape=(ja...  144 us
    unnamed x18, local copies, waits for them, and re-layouts  5.52 us

profile of v3, /device:TPU:27, one launch (start us, length us, event | category | flops | bytes accessed | tf_op | source)
XLA Modules:
  0.0 156.5 jit_solution(10657961697117121129)
XLA Ops:
  0.6 0.0 copy-start.4
  0.6 0.0 copy-start.5
  0.7 0.6 copy-done.4
  1.3 0.0 copy-done.5
  1.3 0.0 copy-start.6
  1.3 0.6 copy-done.6
  2.0 0.6 broadcast_in_dim.24.lab_ref
  2.6 0.6 broadcast_in_dim.26.gap_ref
  3.2 0.0 copy-start.3
  3.2 2.0 %copy.23 = bf16[42,2,8,512]{3,2,0,1:T(8,128)(2,1)} copy(bf16[42,2,8,512]{3,2,1,0:T(8,128)(2,1)} %bitcast.25) | data formatting | bytes 1376256 | tf_op jit(solution)/shard_map/reshape | solution.py:501
  5.2 0.0 copy-done.3
  5.2 1.1 copy.17.dn_ref
  6.3 143.6 %shard_map.137 = (bf16[128,2688]{1,0:T(8,128)(2,1)}, bf16[128,2048]{1,0:T(8,128)(2,1)}, bf16[128,1024]{1,0:T(8,128)(2,1)}, f32[2,16,1344]{2,1,0:T(8,128)}, f32[2,16,512]{2,1,0:T(8,128)}) custom-call(bf16[128,2688]{1,0:T(8,128)(2,1)} %bitcast.26, bf16[128,2048]{1,0:T(8,128)(2,1)} %bitcast.29, bf16[128,1024]{1,0:T(8,128)(2,1)} %bitcast.32, ...), custom_call_target="tpu_custom_call" | custom-call | tf_op jit(solution)/shard_map/pallas_call | solution.py:510
  150.0 0.0 copy-start
  150.0 1.5 copy.21
  151.5 1.0 copy.18
  152.5 0.8 reshape.20
  153.4 0.0 copy-done
  153.4 0.0 copy-start.1
  153.4 0.8 copy.27
  154.2 0.4 copy-done.1
  154.7 0.0 copy-start.2
  154.7 0.8 copy.28
  155.5 0.3 copy-done.2
  155.7 0.7 copy.29
  (2 shorter events, 0.0 us)
Async XLA Ops:
  0.6 0.7 copy-start.4
  0.6 0.7 copy-start.5
  1.3 0.7 copy-start.6
  3.2 2.0 %copy-start.3 = (bf16[2688,16]{0,1:T(8,128)(2,1)S(1)}, bf16[2688,16]{0,1:T(8,128)(2,1)}, u32[]{:S(2)}) copy-start(bf16[2688,16]{0,1:T(8,128)(2,1)} %param.14) | copy-start | bytes 258052
  150.0 3.4 %copy-start = (bf16[128,2688]{1,0:T(8,128)(2,1)S(1)}, bf16[128,2688]{1,0:T(8,128)(2,1)}, u32[]{:S(2)}) copy-start(bf16[128,2688]{1,0:T(8,128)(2,1)} %get-tuple-element.10) | copy-start | bytes 2064388
  153.4 1.3 copy-start.1
  154.7 1.1 copy-start.2

commit v4 on v3

--- a/solution.py
+++ b/solution.py
@@ -260,8 +260,10 @@
         cols = slice(lo, lo + CW)
         half, inner = lo // HALF, lo % HALF
 
-        acc = mm(x_ref[...], wb[half, :, inner:inner + CW], 1, 0) + ADAPT * mm(lowr[...], up_ref[:, cols], 1, 0)
-        vb[0, :, cols] = acc.astype(BF16)
+        if ch % 2 == 0:
+            wide = slice(lo, lo + 2 * CW)
+            acc = mm(x_ref[...], wb[half, :, inner:inner + 2 * CW], 1, 0) + ADAPT * mm(lowr[...], up_ref[:, wide], 1, 0)
+            vb[0, :, wide] = acc.astype(BF16)
         steps = chain(vb, vz_s, vx_s, v_r, vb.at[0], pl.ds(lo, CW), ch)
         v_chains.append(steps)
         steps[0](0)
@@ -490,7 +492,7 @@
     halo = WINDOW // T
     D = min(halo, n - 1)
     L = min(halo // 2, n // 2 - 1)
-    NC = 4
+    NC = 8
     LOG = n.bit_length() - 1
     HALF = width // 2
     pad = R - rows

time: 157 us -> 190 us (1.21)
  Pallas kernels: 144 us -> 176 us
    pallas_call x1, Pallas kernels: 144 us -> 176 us  [shards(): pl.pallas_call(functools.partial(kernel, n, L, D, NC, LOG), out_shape=(ja...]
where the time goes in v4:
time: 190 us; the launch traced here: 189 us
  Pallas kernels  176 us (93%)
  local copies, waits for them, and re-layouts  12.1 us (6%)
    pallas_call x1, Pallas kernels, shards(): pl.pallas_call(functools.partial(kernel, n, L, D, NC, LOG), out_shape=(ja...  176 us
    unnamed x18, local copies, waits for them, and re-layouts  5.52 us

profile of v4, /device:TPU:27, one launch (start us, length us, event | category | flops | bytes accessed | tf_op | source)
XLA Modules:
  0.0 189.2 jit_solution(7340241356226518950)
XLA Ops:
  0.6 0.0 copy-start.4
  0.6 0.0 copy-start.5
  0.7 0.6 copy-done.4
  1.3 0.0 copy-done.5
  1.3 0.0 copy-start.6
  1.3 0.6 copy-done.6
  2.0 0.6 broadcast_in_dim.24.lab_ref
  2.6 0.6 broadcast_in_dim.26.gap_ref
  3.2 0.0 copy-start.3
  3.2 2.0 %copy.23 = bf16[42,2,8,512]{3,2,0,1:T(8,128)(2,1)} copy(bf16[42,2,8,512]{3,2,1,0:T(8,128)(2,1)} %bitcast.25) | data formatting | bytes 1376256 | tf_op jit(solution)/shard_map/reshape | solution.py:503
  5.2 0.0 copy-done.3
  5.2 1.1 copy.17.dn_ref
  6.3 176.4 %shard_map.137 = (bf16[128,2688]{1,0:T(8,128)(2,1)}, bf16[128,2048]{1,0:T(8,128)(2,1)}, bf16[128,1024]{1,0:T(8,128)(2,1)}, f32[2,16,1344]{2,1,0:T(8,128)}, f32[2,16,512]{2,1,0:T(8,128)}) custom-call(bf16[128,2688]{1,0:T(8,128)(2,1)} %bitcast.26, bf16[128,2048]{1,0:T(8,128)(2,1)} %bitcast.29, bf16[128,1024]{1,0:T(8,128)(2,1)} %bitcast.32, ...), custom_call_target="tpu_custom_call" | custom-call | tf_op jit(solution)/shard_map/pallas_call | solution.py:512
  182.7 0.0 copy-start
  182.7 1.5 copy.21
  184.3 1.0 copy.18
  185.3 0.8 reshape.20
  186.1 0.0 copy-done
  186.1 0.0 copy-start.1
  186.1 0.8 copy.27
  187.0 0.4 copy-done.1
  187.4 0.0 copy-start.2
  187.4 0.8 copy.28
  188.2 0.3 copy-done.2
  188.5 0.7 copy.29
  (2 shorter events, 0.0 us)
Async XLA Ops:
  0.6 0.7 copy-start.4
  0.6 0.7 copy-start.5
  1.3 0.7 copy-start.6
  3.2 2.0 %copy-start.3 = (bf16[2688,16]{0,1:T(8,128)(2,1)S(1)}, bf16[2688,16]{0,1:T(8,128)(2,1)}, u32[]{:S(2)}) copy-start(bf16[2688,16]{0,1:T(8,128)(2,1)} %param.14) | copy-start | bytes 258052
  182.7 3.4 %copy-start = (bf16[128,2688]{1,0:T(8,128)(2,1)S(1)}, bf16[128,2688]{1,0:T(8,128)(2,1)}, u32[]{:S(2)}) copy-start(bf16[128,2688]{1,0:T(8,128)(2,1)} %get-tuple-element.10) | copy-start | bytes 2064388
  186.1 1.3 copy-start.1
  187.4 1.1 copy-start.2
